TPU v7x, 256 devices: a whole 4x4x8 slice. The times are simulated.
256 devices in a mesh: grp: 8 (over x, core), row: 4 (over y), col: 8 (over z).
Axes of the slice: x: 4, y: 4, z: 8, core: 2. Of those that a mesh axis runs over, the one named last changes fastest.
Arguments:
- amplitudes: bfloat16 [8, 2048, 4608], P('grp', ('row', 'col')), may hold values from -6 to 6
- integrals: bfloat16 [8, 4608, 12288], P('grp', None, ('row', 'col')), may hold values from -0.0546875 to 0.0546875
- block_tiles: int32 [8], replicated, may hold values from 1 to 36, 96 in all
- assign: int32 [8], replicated, may hold values from 0 to 7, each once
Outputs:
- residual: float32 [2048, 12288], P('grp', ('row', 'col'))
Inputs may be any that keep to these rules, and one draw needn't show every extreme that they name: `block_tiles`: the entries sum to 96; the largest is exactly 36. Each block b is held in slot assign[b]; the slots form a permutation, and consecutive slots belong to one group in the order of grp.
All inputs are finite; a program needn't handle non-finite values.
Results may differ from a plain program's by a relative error of at most 0.0003.
Values may be sent and summed in bfloat16 or wider, within the bound.
No kernel may reach another device: no remote copies, remote signals or barrier semaphores. Data moves between devices by JAX's collectives and lax.ppermute only.
A program may use at most 128 MiB of HBM per device.

v0:
```python
import functools

import jax
import jax.numpy as jnp
from jax import lax
from jax.experimental import pallas as pl
from jax.experimental.pallas import tpu as pltpu
from jax.sharding import PartitionSpec as P

TP = 128
ANY = pl.BlockSpec(memory_space=pl.ANY)
SMEM = pl.BlockSpec(memory_space=pltpu.SMEM)
VMEM = pl.BlockSpec(memory_space=pltpu.VMEM)


def balance(tiles_ref, assign_ref, held_ref, block_ref, groups):
    for b in range(groups):
        held_ref[assign_ref[b]] = tiles_ref[b]
        block_ref[assign_ref[b]] = b
    chips = groups // 2
    held = [held_ref[s] for s in range(groups)]
    total = [held[2 * x] + held[2 * x + 1] for x in range(chips)]
    share = 0
    for x in range(chips):
        share = share + total[x]
    share = share // chips
    running, prefix = 0, []
    for x in range(chips):
        running = running + total[x] - share
        prefix.append(running)
    high = functools.reduce(jnp.maximum, prefix)
    low = functools.reduce(jnp.minimum, prefix)
    middle = lax.shift_right_arithmetic(high + low, jnp.int32(1))
    flow = [p - middle for p in prefix]
    right = [jnp.maximum(flow[x], 0) for x in range(chips)]
    left = [jnp.maximum(-flow[(x - 1) % chips], 0) for x in range(chips)]
    return held, total, right, left


def half(n, core):
    first = lax.shift_right_arithmetic(n + 1, jnp.int32(1))
    if isinstance(core, int):
        return (0, first) if core == 0 else (first, n - first)
    return jnp.where(core == 0, 0, first), jnp.where(core == 0, first, n - first)


def pick(values, index):
    out = values[0]
    for i in range(1, len(values)):
        out = jnp.where(index == i, values[i], out)
    return out


def plan(x, core, total, right, left, own):
    chips = len(total)
    if isinstance(x, int):
        xl, xr = (x - 1) % chips, (x + 1) % chips
        from_left, from_right = right[xl], left[xr]
        left_first, kept_first = total[xl] - right[xl], left[x]
    else:
        xl, xr = lax.rem(x + chips - 1, chips), lax.rem(x + 1, chips)
        from_left, from_right = pick(right, xl), pick(left, xr)
        left_first, kept_first = pick(total, xl) - from_left, pick(left, x)
    l0, nl = half(from_left, core)
    r0, nr = half(from_right, core)
    first = own - half(from_left, 0)[1] - half(from_right, 0)[1]
    k0 = core * first if isinstance(core, int) else jnp.where(core == 0, 0, first)
    return (xl, left_first + l0, nl), (xr, r0, nr), (x, kept_first + k0, own - nl - nr)


def pack_amplitudes(groups, own, tiles_ref, assign_ref, src_ref, out_ref, held_ref, block_ref):
    held, total, right, left = balance(tiles_ref, assign_ref, held_ref, block_ref, groups)
    blocks = [block_ref[s] for s in range(groups)]
    for g in range(groups):
        place = 0
        for chip, start, count in plan(g // 2, g % 2, total, right, left, own):
            n0 = jnp.clip(held[2 * chip] - start, 0, count)
            second = jnp.maximum(start - held[2 * chip], 0)
            for block, tile, many in ((blocks[2 * chip], start, n0), (blocks[2 * chip + 1], second, count - n0)):

                def move(i, carry, block=block, tile=tile, place=place):
                    into = pl.ds(pl.multiple_of((place + i) * TP, TP), TP)
                    out_ref[g, :, into] = src_ref[block, :, pl.ds(pl.multiple_of((tile + i) * TP, TP), TP)]
                    return carry

                lax.fori_loop(0, many, move, 0)
                place = place + many


def tile_rows(index):
    return pl.ds(pl.multiple_of(index * TP, TP), TP)


def copy_run(border, core, start, count, mine_ref, other_ref, out_ref, place):
    lower = jnp.clip(border - start, 0, count)
    for upper, tile, many, at in ((0, start, lower, place), (1, jnp.maximum(start - border, 0), count - lower, place + lower)):
        for source, here in ((mine_ref, core == upper), (other_ref, core != upper)):

            def move(i, carry, source=source, tile=tile, at=at):
                out_ref[tile_rows(at + i), :] = source[tile_rows(tile + i), :]
                return carry

            lax.fori_loop(0, jnp.where(here, many, 0), move, 0)


def send_tiles(groups, own, tiles_ref, assign_ref, mine_ref, other_ref, right_ref, left_ref, held_ref, block_ref):
    held, total, right, left = balance(tiles_ref, assign_ref, held_ref, block_ref, groups)
    group = lax.axis_index("grp")
    x, core = lax.div(group, 2), lax.rem(group, 2)
    border = pick(held[0::2], x)
    go_right, go_left = pick(right, x), pick(left, x)
    r0, nr = half(go_right, core)
    l0, nl = half(go_left, core)
    copy_run(border, core, pick(total, x) - go_right + r0, nr, mine_ref, other_ref, right_ref, 0)
    copy_run(border, core, l0, nl, mine_ref, other_ref, left_ref, 0)


def join_tiles(groups, own, tiles_ref, assign_ref, mine_ref, other_ref, fl_ref, fr_ref, out_ref, held_ref, block_ref):
    held, total, right, left = balance(tiles_ref, assign_ref, held_ref, block_ref, groups)
    group = lax.axis_index("grp")
    x, core = lax.div(group, 2), lax.rem(group, 2)
    border = pick(held[0::2], x)
    (_, _, nl), (_, _, nr), (_, start, count) = plan(x, core, total, right, left, own)
    for source, many, place in ((fl_ref, nl, 0), (fr_ref, nr, nl)):

        def move(i, carry, source=source, place=place):
            out_ref[tile_rows(place + i), :] = source[tile_rows(i), :]
            return carry

        lax.fori_loop(0, many, move, 0)
    copy_run(border, core, start, count, mine_ref, other_ref, out_ref, nl + nr)


def multiply(ny, nz, rows, *refs):
    zs, ys, (b_ref, keep_ref, send_ref) = refs[:ny], refs[ny : ny + nz], refs[ny + nz :]
    group, y, z = lax.axis_index("grp"), lax.axis_index("row"), lax.axis_index("col")
    x, core = lax.div(group, 2), lax.rem(group, 2)
    wide = zs[0].shape[1]
    part = rows * nz // 2
    for r in range(ny):
        d = lax.rem(y + r - x + ny, ny)
        out = jnp.dot(zs[r][...], b_ref[:wide, :], preferred_element_type=jnp.float32)
        keep_ref[d] = jnp.where(core == 0, out[:part], out[part:])
        send_ref[d] = jnp.where(core == 0, out[part:], out[:part])
    for r in range(nz):
        at = lax.rem(z + r, nz)
        side = lax.div(at, nz // 2)
        into = pl.ds(pl.multiple_of(lax.rem(at, nz // 2) * rows, rows), rows)
        out = jnp.dot(ys[r][...], b_ref[wide:, :], preferred_element_type=jnp.float32)
        for ref, here in ((keep_ref, side == core), (send_ref, side != core)):

            @pl.when(here)
            def _(ref=ref, out=out):
                for q in range(ny):
                    d = lax.rem(q - x + ny, ny)
                    ref[d, into, :] += out[q * rows : (q + 1) * rows]


def steps(n):
    return [(i, (i + 1) % n) for i in range(n)], [(i, (i - 1) % n) for i in range(n)]


def ring(block, axis, n):
    up, down = steps(n)
    out = [block] * n
    a = b = block
    for s in range(1, n // 2):
        a, b = lax.ppermute(a, axis, up), lax.ppermute(b, axis, down)
        out[n - s], out[s] = a, b
    h = block.shape[0] // 2
    ta, tb = lax.ppermute(a[:h], axis, up), lax.ppermute(b[h:], axis, down)
    out[n // 2] = jnp.concatenate([ta, tb], axis=0)
    return out


def body(amplitudes, integrals, block_tiles, assign):
    groups = assign.shape[0]
    _, rows, cap = amplitudes.shape
    cols = integrals.shape[2]
    ny, nz = lax.axis_size("row"), lax.axis_size("col")
    own = 12
    wide = own * TP
    split = 7 * TP
    small = [pltpu.SMEM((groups,), jnp.int32)] * 2
    swap = [(g, g ^ 1) for g in range(groups)]
    up = [(g, (g + 2) % groups) for g in range(groups)]
    down = [(g, (g - 2) % groups) for g in range(groups)]
    limit = pltpu.CompilerParams(vmem_limit_bytes=24 * 2**20)

    mine = integrals[0]
    other = lax.ppermute(mine, "grp", swap)
    moved = lax.all_to_all(amplitudes[0].reshape(groups, rows // groups, cap), "grp", 0, 0, tiled=True)
    packed = pl.pallas_call(
        functools.partial(pack_amplitudes, groups, own),
        out_shape=jax.ShapeDtypeStruct((groups, rows // groups, wide), jnp.bfloat16),
        in_specs=[SMEM, SMEM, VMEM],
        out_specs=VMEM,
        scratch_shapes=small,
    )(block_tiles, assign, moved)
    piece = lax.all_to_all(packed, "grp", 0, 0, tiled=True).reshape(rows, wide)

    sends = jax.ShapeDtypeStruct((wide, cols), jnp.bfloat16)
    to_right, to_left = pl.pallas_call(
        functools.partial(send_tiles, groups, own),
        out_shape=(sends, sends),
        in_specs=[SMEM, SMEM, VMEM, VMEM],
        out_specs=(VMEM, VMEM),
        scratch_shapes=small,
        compiler_params=limit,
    )(block_tiles, assign, mine, other)
    from_left = lax.ppermute(to_right, "grp", up)
    from_right = lax.ppermute(to_left, "grp", down)
    held = pl.pallas_call(
        functools.partial(join_tiles, groups, own),
        out_shape=sends,
        in_specs=[SMEM, SMEM, VMEM, VMEM, VMEM, VMEM],
        out_specs=VMEM,
        scratch_shapes=small,
        compiler_params=limit,
    )(block_tiles, assign, mine, other, from_left, from_right)

    y_line = lax.all_gather(piece[:, split:], "row", axis=0, tiled=True)
    z_line = lax.all_gather(piece[:, :split], "col", axis=0, tiled=True)
    zs = ring(z_line, "row", ny)
    ys = ring(y_line, "col", nz)
    half_rows = rows * nz // 2
    kept = jax.ShapeDtypeStruct((ny, half_rows, cols), jnp.float32)
    keep, send = pl.pallas_call(
        functools.partial(multiply, ny, nz, rows),
        out_shape=(kept, kept),
        in_specs=[VMEM] * (ny + nz + 1),
        out_specs=(VMEM, VMEM),
        compiler_params=pltpu.CompilerParams(vmem_limit_bytes=32 * 2**20),
    )(*zs, *ys, held)

    p = keep + lax.ppermute(send, "grp", swap)
    h = half_rows // 2
    a = lax.ppermute(jnp.concatenate([p[2, :h], p[1, h:]]), "grp", up)
    b = lax.ppermute(jnp.concatenate([p[2, h:], p[3, :h]]), "grp", down)
    a2 = lax.ppermute(p[1, :h] + a[:h], "grp", up)
    b2 = lax.ppermute(p[3, h:] + b[:h], "grp", down)
    return p[0] + jnp.concatenate([a2, a[h:]]) + jnp.concatenate([b[h:], b2])


def solution(mesh):
    in_specs = (P("grp", ("row", "col"), None), P("grp", None, ("row", "col")), P(), P())
    out_specs = P("grp", ("row", "col"))
    return jax.shard_map(body, mesh=mesh, in_specs=in_specs, out_specs=out_specs, check_vma=False)
```

profile of v0, /device:TPU:1, one launch (start us, length us, event | category | flops | bytes accessed | tf_op | source)
XLA Modules:
  0.0 148.8 jit_solution(3118724671116245694)
XLA Ops:
  0.0 3.2 %collective-permute-start.12 = (bf16[4608,384]{1,0:T(8,128)(2,1)}, bf16[4608,384]{1,0:T(8,128)(2,1)}, u32[]{:S(2)}, u32[]{:S(2)}) collective-permute-start(bf16[4608,384]{1,0:T(8,128)(2,1)} %bitcast.25), channel_id=1, source_target_pairs={{0,32},{32,0},{64,96},{96,64},{128,160},{160,128},{192,224},{224,1... | collective-permute-start | bytes 10616840 | tf_op jit(solution)/shard_map/ppermute | solution.py:191
  3.2 0.0 copy-start
  3.2 14.8 %all_to_all.10.src_ref = bf16[8,8,4608]{2,1,0:T(8,128)(2,1)} all-to-all(bf16[8,8,4608]{2,1,0:T(8,128)(2,1)} %bitcast.30), channel_id=1, replica_groups=mesh['grp'=8,'row'=4,'col'=8] {'grp'}, dimensions={0} | all-to-all | bytes 1179648 | tf_op jit(solution)/shard_map/all_to_all | solution.py:192
  18.0 0.0 copy-start.1
  18.0 0.0 copy-start.2
  18.0 2.9 %shard_map.46 = bf16[8,8,1536]{2,1,0:T(8,128)(2,1)} custom-call(s32[8]{0:T(128)} %tiles_ref.5, s32[8]{0:T(128)} %assign_ref.5, bf16[8,8,4608]{2,1,0:T(8,128)(2,1)} %all_to_all.10.src_ref), custom_call_target="tpu_custom_call" | custom-call | tf_op jit(solution)/shard_map/pallas_call | solution.py:193
  20.9 9.9 %all_to_all.11 = bf16[8,8,1536]{2,1,0:T(8,128)(2,1)S(1)} all-to-all(bf16[8,8,1536]{2,1,0:T(8,128)(2,1)} %shard_map.46), channel_id=1, replica_groups=mesh['grp'=8,'row'=4,'col'=8] {'grp'}, dimensions={0} | all-to-all | bytes 393216 | tf_op jit(solution)/shard_map/all_to_all | solution.py:200
  30.9 10.0 %all_gather.7.refs_4_ = bf16[256,640]{1,0:T(8,128)(2,1)S(1)} all-gather(bf16[64,640]{1,0:T(8,128)(2,1)S(1)} %slice.71), channel_id=1, replica_groups=mesh['grp'=8,'row'=4,'col'=8] {'row'}, dimensions={0}, use_global_device_ids=true | all-gather | bytes 409600 | tf_op jit(solution)/shard_map/all_gather | solution.py:222
  40.9 1.3 collective-permute-start.7
  42.2 26.3 %all_gather.6.refs_0_ = bf16[512,896]{1,0:T(8,128)(2,1)S(1)} all-gather(bf16[64,896]{1,0:T(8,128)(2,1)S(1)} %slice.68), channel_id=1, replica_groups=mesh['grp'=8,'row'=4,'col'=8] {'col'}, dimensions={0}, use_global_device_ids=true | all-gather | bytes 1032192 | tf_op jit(solution)/shard_map/all_gather | solution.py:223
  68.5 0.0 collective-permute-start.1
  68.5 1.2 collective-permute-start.4
  69.7 2.7 %collective-permute-start = (bf16[512,896]{1,0:T(8,128)(2,1)S(1)}, bf16[512,896]{1,0:T(8,128)(2,1)S(1)}, u32[]{:S(2)}, u32[]{:S(2)}) collective-permute-start(bf16[512,896]{1,0:T(8,128)(2,1)S(1)} %all_gather.6.refs_0_), channel_id=1, source_target_pairs={{0,24},{8,0},{16,8},{24,16},{1,25},{9,1},{17,9},{25,17},{2,26},{10... | collective-permute-start | bytes 2752520 | tf_op jit(solution)/shard_map/ppermute | solution.py:168
  72.4 0.0 collective-permute-done.7.refs_11_
  72.4 0.3 collective-permute-start.8
  72.7 2.6 %collective-permute-done.4.refs_5_ = bf16[256,640]{1,0:T(8,128)(2,1)S(1)} collective-permute-done((bf16[256,640]{1,0:T(8,128)(2,1)S(1)}, bf16[256,640]{1,0:T(8,128)(2,1)S(1)}, u32[]{:S(2)}, u32[]{:S(2)}) %collective-permute-start.4) | collective-permute-done | bytes 327712 | tf_op jit(solution)/shard_map/ppermute | solution.py:168
  75.3 3.0 %collective-permute-start.5 = (bf16[256,640]{1,0:T(8,128)(2,1)S(1)}, bf16[256,640]{1,0:T(8,128)(2,1)S(1)}, u32[]{:S(2)}, u32[]{:S(2)}) collective-permute-start(bf16[256,640]{1,0:T(8,128)(2,1)S(1)} %collective-permute-done.4.refs_5_), channel_id=1, source_target_pairs={{0,7},{1,0},{2,1},{3,2},{4,3},{5,4},{6,5},{7,6},{8,15},{9,8},{10,9... | collective-permute-start | bytes 983048 | tf_op jit(solution)/shard_map/ppermute | solution.py:168
  78.3 0.0 collective-permute-done.12.other_ref
  78.3 0.0 copy-done
  78.3 0.0 copy-done.1
  78.3 0.0 copy-done.2
  78.3 2.1 %shard_map.47 = (bf16[1536,384]{1,0:T(8,128)(2,1)S(1)}, bf16[1536,384]{1,0:T(8,128)(2,1)S(1)}) custom-call(s32[8]{0:T(128)S(1)} %copy-done.1, s32[8]{0:T(128)S(1)} %copy-done.2, bf16[4608,384]{1,0:T(8,128)(2,1)S(1)} %bitcast.26, bf16[4608,384]{1,0:T(8,128)(2,1)} %collective-permute-done.12.other_ref), custom_call_target="tpu_custom_call" | custom-call | tf_op jit(solution)/shard_map/pallas_call | solution.py:203
  80.4 0.4 collective-permute-start.13
  80.8 0.0 collective-permute-done.8.refs_10_
  80.8 2.4 %collective-permute-start.14 = (bf16[1536,384]{1,0:T(8,128)(2,1)S(1)}, bf16[1536,384]{1,0:T(8,128)(2,1)S(1)}, u32[]{:S(2)}, u32[]{:S(2)}) collective-permute-start(bf16[1536,384]{1,0:T(8,128)(2,1)S(1)} %get-tuple-element.10), channel_id=1, source_target_pairs={{0,192},{32,224},{64,0},{96,32},{128,64},{160,96},{192,128},{224,1... | collective-permute-start | bytes 3538952 | tf_op jit(solution)/shard_map/ppermute | solution.py:212
  83.2 0.5 collective-permute-done.5.refs_6_
  83.7 0.9 collective-permute-start.9
  84.6 0.0 collective-permute-done.1.refs_3_
  84.7 2.5 %collective-permute-start.6 = (bf16[256,640]{1,0:T(8,128)(2,1)S(1)}, bf16[256,640]{1,0:T(8,128)(2,1)S(1)}, u32[]{:S(2)}, u32[]{:S(2)}) collective-permute-start(bf16[256,640]{1,0:T(8,128)(2,1)S(1)} %collective-permute-done.5.refs_6_), channel_id=1, source_target_pairs={{0,7},{1,0},{2,1},{3,2},{4,3},{5,4},{6,5},{7,6},{8,15},{9,8},{10,9... | collective-permute-start | bytes 983048 | tf_op jit(solution)/shard_map/ppermute | solution.py:168
  87.2 0.0 collective-permute-done.refs_1_
  87.2 0.8 collective-permute-start.2
  88.0 5.4 %collective-permute-done.9.refs_9_ = bf16[256,640]{1,0:T(8,128)(2,1)S(1)} collective-permute-done((bf16[256,640]{1,0:T(8,128)(2,1)S(1)}, bf16[256,640]{1,0:T(8,128)(2,1)S(1)}, u32[]{:S(2)}, u32[]{:S(2)}) %collective-permute-start.9) | collective-permute-done | bytes 327712 | tf_op jit(solution)/shard_map/ppermute | solution.py:168
  93.4 1.3 collective-permute-start.3
  94.7 0.0 collective-permute-done.6.refs_7_
  94.7 1.6 %collective-permute-start.10 = (bf16[128,640]{1,0:T(8,128)(2,1)S(1)}, bf16[128,640]{1,0:T(8,128)(2,1)S(1)}, u32[]{:S(2)}, u32[]{:S(2)}) collective-permute-start(bf16[128,640]{1,0:T(8,128)(2,1)S(1)} %slice.72), channel_id=1, source_target_pairs={{0,1},{1,2},{2,3},{3,4},{4,5},{5,6},{6,7},{7,0},{8,9},{9,10},{10,1... | collective-permute-start | bytes 491528 | tf_op jit(solution)/shard_map/ppermute | solution.py:171
  96.4 4.6 %collective-permute-done.10 = bf16[128,640]{1,0:T(8,128)(2,1)S(1)} collective-permute-done((bf16[128,640]{1,0:T(8,128)(2,1)S(1)}, bf16[128,640]{1,0:T(8,128)(2,1)S(1)}, u32[]{:S(2)}, u32[]{:S(2)}) %collective-permute-start.10) | collective-permute-done | bytes 163872 | tf_op jit(solution)/shard_map/ppermute | solution.py:171
  101.0 0.0 collective-permute-start.11
  101.0 5.0 %collective-permute-done.11 = bf16[128,640]{1,0:T(8,128)(2,1)S(1)} collective-permute-done((bf16[128,640]{1,0:T(8,128)(2,1)S(1)}, bf16[128,640]{1,0:T(8,128)(2,1)S(1)}, u32[]{:S(2)}, u32[]{:S(2)}) %collective-permute-start.11) | collective-permute-done | bytes 163872 | tf_op jit(solution)/shard_map/ppermute | solution.py:171
  106.1 0.0 collective-permute-done.2
  106.1 0.0 collective-permute-done.3
  106.1 0.1 pad_maximum_fusion.refs_2_
  106.2 0.0 collective-permute-done.13.fl_ref
  106.2 0.0 collective-permute-done.14.fr_ref
  106.2 2.3 %shard_map.48.refs_12_ = bf16[1536,384]{1,0:T(8,128)(2,1)S(1)} custom-call(s32[8]{0:T(128)S(1)} %copy-done.1, s32[8]{0:T(128)S(1)} %copy-done.2, bf16[4608,384]{1,0:T(8,128)(2,1)S(1)} %bitcast.27, bf16[4608,384]{1,0:T(8,128)(2,1)} %collective-permute-done.12.other_ref, bf16[1536,384]{1,0:T(8,128)(2,1)S(1)} %collective-permute-done.13.fl_ref, ...), custom_call_target="tpu_custom_call" | custom-call | tf_op jit(solution)/shard_map/pallas_call | solution.py:213
  108.5 5.3 %shard_map.49 = (f32[4,256,384]{2,1,0:T(8,128)S(1)}, f32[4,256,384]{2,1,0:T(8,128)S(1)}) custom-call(bf16[512,896]{1,0:T(8,128)(2,1)S(1)} %all_gather.6.refs_0_, bf16[512,896]{1,0:T(8,128)(2,1)S(1)} %collective-permute-done.refs_1_, bf16[512,896]{1,0:T(8,128)(2,1)S(1)} %pad_maximum_fusion.refs_2_, bf16[512,896]{1,0:T(8,128)(2,1)S(1)} %collective-permute-done.1.refs_3_, ...), custom_call_target="tpu_custom_call" | custom-call | tf_op jit(solution)/shard_map/pallas_call | solution.py:228
  113.8 12.6 %collective-permute-start.15 = (f32[4,256,384]{2,1,0:T(8,128)S(1)}, f32[4,256,384]{2,1,0:T(8,128)S(1)}, u32[]{:S(2)}, u32[]{:S(2)}) collective-permute-start(f32[4,256,384]{2,1,0:T(8,128)S(1)} %get-tuple-element.12), channel_id=1, source_target_pairs={{0,32},{32,0},{64,96},{96,64},{128,160},{160,128},{192,224},{224,1... | collective-permute-start | bytes 4718600 | tf_op jit(solution)/shard_map/ppermute | solution.py:236
  126.4 3.0 %collective-permute-done.15 = f32[4,256,384]{2,1,0:T(8,128)S(1)} collective-permute-done((f32[4,256,384]{2,1,0:T(8,128)S(1)}, f32[4,256,384]{2,1,0:T(8,128)S(1)}, u32[]{:S(2)}, u32[]{:S(2)}) %collective-permute-start.15) | collective-permute-done | bytes 1572896 | tf_op jit(solution)/shard_map/ppermute | solution.py:236
  129.4 0.3 add.15
  129.7 0.1 slice_bitcast_fusion.3
  129.8 0.4 collective-permute-start.16
  130.2 2.5 %collective-permute-start.18 = (f32[256,384]{1,0:T(8,128)S(1)}, f32[256,384]{1,0:T(8,128)S(1)}, u32[]{:S(2)}, u32[]{:S(2)}) collective-permute-start(f32[256,384]{1,0:T(8,128)S(1)} %pad_maximum_fusion.2), channel_id=1, source_target_pairs={{0,192},{32,224},{64,0},{96,32},{128,64},{160,96},{192,128},{224,1... | collective-permute-start | bytes 1179656 | tf_op jit(solution)/shard_map/ppermute | solution.py:239
  132.7 8.8 %collective-permute-done.16 = f32[256,384]{1,0:T(8,128)S(1)} collective-permute-done((f32[256,384]{1,0:T(8,128)S(1)}, f32[256,384]{1,0:T(8,128)S(1)}, u32[]{:S(2)}, u32[]{:S(2)}) %collective-permute-start.16) | collective-permute-done | bytes 393248 | tf_op jit(solution)/shard_map/ppermute | solution.py:238
  141.4 0.0 collective-permute-done.18
  141.4 0.1 slice_add_fusion
  141.5 0.1 collective-permute-start.17
  141.6 2.7 %collective-permute-start.19 = (f32[128,384]{1,0:T(8,128)S(1)}, f32[128,384]{1,0:T(8,128)S(1)}, u32[]{:S(2)}, u32[]{:S(2)}) collective-permute-start(f32[128,384]{1,0:T(8,128)S(1)} %get-tuple-element.13), channel_id=1, source_target_pairs={{0,192},{32,224},{64,0},{96,32},{128,64},{160,96},{192,128},{224,1... | collective-permute-start | bytes 589832 | tf_op jit(solution)/shard_map/ppermute | solution.py:241
  144.2 3.7 %collective-permute-done.17 = f32[128,384]{1,0:T(8,128)S(1)} collective-permute-done((f32[128,384]{1,0:T(8,128)S(1)}, f32[128,384]{1,0:T(8,128)S(1)}, u32[]{:S(2)}, u32[]{:S(2)}) %collective-permute-start.17) | collective-permute-done | bytes 196640 | tf_op jit(solution)/shard_map/ppermute | solution.py:240
  148.0 0.0 collective-permute-done.19
  148.0 0.8 fusion.1
  (9 shorter events, 0.2 us)
Async XLA Ops:
  0.0 78.3 %collective-permute-start.12 = (bf16[4608,384]{1,0:T(8,128)(2,1)}, bf16[4608,384]{1,0:T(8,128)(2,1)}, u32[]{:S(2)}, u32[]{:S(2)}) collective-permute-start(bf16[4608,384]{1,0:T(8,128)(2,1)} %bitcast.25), channel_id=1, source_target_pairs={{0,32},{32,0},{64,96},{96,64},{128,160},{160,128},{192,224},{224,1... | collective-permute-start | bytes 10616840 | tf_op jit(solution)/shard_map/ppermute | solution.py:191
  3.2 75.0 %copy-start = (bf16[1,4608,384]{2,1,0:T(8,128)(2,1)S(1)}, bf16[1,4608,384]{2,1,0:T(8,128)(2,1)}, u32[]{:S(2)}) copy-start(bf16[1,4608,384]{2,1,0:T(8,128)(2,1)} %param.5) | copy-start | bytes 10616836
  18.0 60.2 %copy-start.1 = (s32[8]{0:T(128)S(1)}, s32[8]{0:T(128)}, u32[]{:S(2)}) copy-start(s32[8]{0:T(128)} %tiles_ref.5) | copy-start | bytes 100
  18.0 60.2 %copy-start.2 = (s32[8]{0:T(128)S(1)}, s32[8]{0:T(128)}, u32[]{:S(2)}) copy-start(s32[8]{0:T(128)} %assign_ref.5) | copy-start | bytes 100
  40.9 31.5 %collective-permute-start.7 = (bf16[256,640]{1,0:T(8,128)(2,1)S(1)}, bf16[256,640]{1,0:T(8,128)(2,1)S(1)}, u32[]{:S(2)}, u32[]{:S(2)}) collective-permute-start(bf16[256,640]{1,0:T(8,128)(2,1)S(1)} %all_gather.7.refs_4_), channel_id=1, source_target_pairs={{0,1},{1,2},{2,3},{3,4},{4,5},{5,6},{6,7},{7,0},{8,9},{9,10},{10,1... | collective-permute-start | bytes 983048 | tf_op jit(solution)/shard_map/ppermute | solution.py:168
  68.5 16.1 %collective-permute-start.1 = (bf16[512,896]{1,0:T(8,128)(2,1)S(1)}, bf16[512,896]{1,0:T(8,128)(2,1)S(1)}, u32[]{:S(2)}, u32[]{:S(2)}) collective-permute-start(bf16[512,896]{1,0:T(8,128)(2,1)S(1)} %all_gather.6.refs_0_), channel_id=1, source_target_pairs={{0,8},{8,16},{16,24},{24,0},{1,9},{9,17},{17,25},{25,1},{2,10},{10... | collective-permute-start | bytes 2752520 | tf_op jit(solution)/shard_map/ppermute | solution.py:168
  68.5 6.8 %collective-permute-start.4 = (bf16[256,640]{1,0:T(8,128)(2,1)S(1)}, bf16[256,640]{1,0:T(8,128)(2,1)S(1)}, u32[]{:S(2)}, u32[]{:S(2)}) collective-permute-start(bf16[256,640]{1,0:T(8,128)(2,1)S(1)} %all_gather.7.refs_4_), channel_id=1, source_target_pairs={{0,7},{1,0},{2,1},{3,2},{4,3},{5,4},{6,5},{7,6},{8,15},{9,8},{10,9... | collective-permute-start | bytes 983048 | tf_op jit(solution)/shard_map/ppermute | solution.py:168
  69.7 17.5 %collective-permute-start = (bf16[512,896]{1,0:T(8,128)(2,1)S(1)}, bf16[512,896]{1,0:T(8,128)(2,1)S(1)}, u32[]{:S(2)}, u32[]{:S(2)}) collective-permute-start(bf16[512,896]{1,0:T(8,128)(2,1)S(1)} %all_gather.6.refs_0_), channel_id=1, source_target_pairs={{0,24},{8,0},{16,8},{24,16},{1,25},{9,1},{17,9},{25,17},{2,26},{10... | collective-permute-start | bytes 2752520 | tf_op jit(solution)/shard_map/ppermute | solution.py:168
  72.4 8.4 %collective-permute-start.8 = (bf16[256,640]{1,0:T(8,128)(2,1)S(1)}, bf16[256,640]{1,0:T(8,128)(2,1)S(1)}, u32[]{:S(2)}, u32[]{:S(2)}) collective-permute-start(bf16[256,640]{1,0:T(8,128)(2,1)S(1)} %collective-permute-done.7.refs_11_), channel_id=1, source_target_pairs={{0,1},{1,2},{2,3},{3,4},{4,5},{5,6},{6,7},{7,0},{8,9},{9,10},{10,1... | collective-permute-start | bytes 983048 | tf_op jit(solution)/shard_map/ppermute | solution.py:168
  75.3 8.4 %collective-permute-start.5 = (bf16[256,640]{1,0:T(8,128)(2,1)S(1)}, bf16[256,640]{1,0:T(8,128)(2,1)S(1)}, u32[]{:S(2)}, u32[]{:S(2)}) collective-permute-start(bf16[256,640]{1,0:T(8,128)(2,1)S(1)} %collective-permute-done.4.refs_5_), channel_id=1, source_target_pairs={{0,7},{1,0},{2,1},{3,2},{4,3},{5,4},{6,5},{7,6},{8,15},{9,8},{10,9... | collective-permute-start | bytes 983048 | tf_op jit(solution)/shard_map/ppermute | solution.py:168
  80.4 25.7 %collective-permute-start.13 = (bf16[1536,384]{1,0:T(8,128)(2,1)S(1)}, bf16[1536,384]{1,0:T(8,128)(2,1)S(1)}, u32[]{:S(2)}, u32[]{:S(2)}) collective-permute-start(bf16[1536,384]{1,0:T(8,128)(2,1)S(1)} %get-tuple-element.9), channel_id=1, source_target_pairs={{0,64},{32,96},{64,128},{96,160},{128,192},{160,224},{192,0},{224,... | collective-permute-start | bytes 3538952 | tf_op jit(solution)/shard_map/ppermute | solution.py:211
  80.8 25.4 %collective-permute-start.14 = (bf16[1536,384]{1,0:T(8,128)(2,1)S(1)}, bf16[1536,384]{1,0:T(8,128)(2,1)S(1)}, u32[]{:S(2)}, u32[]{:S(2)}) collective-permute-start(bf16[1536,384]{1,0:T(8,128)(2,1)S(1)} %get-tuple-element.10), channel_id=1, source_target_pairs={{0,192},{32,224},{64,0},{96,32},{128,64},{160,96},{192,128},{224,1... | collective-permute-start | bytes 3538952 | tf_op jit(solution)/shard_map/ppermute | solution.py:212
  83.7 9.6 %collective-permute-start.9 = (bf16[256,640]{1,0:T(8,128)(2,1)S(1)}, bf16[256,640]{1,0:T(8,128)(2,1)S(1)}, u32[]{:S(2)}, u32[]{:S(2)}) collective-permute-start(bf16[256,640]{1,0:T(8,128)(2,1)S(1)} %collective-permute-done.8.refs_10_), channel_id=1, source_target_pairs={{0,1},{1,2},{2,3},{3,4},{4,5},{5,6},{6,7},{7,0},{8,9},{9,10},{10,1... | collective-permute-start | bytes 983048 | tf_op jit(solution)/shard_map/ppermute | solution.py:168
  84.7 10.1 %collective-permute-start.6 = (bf16[256,640]{1,0:T(8,128)(2,1)S(1)}, bf16[256,640]{1,0:T(8,128)(2,1)S(1)}, u32[]{:S(2)}, u32[]{:S(2)}) collective-permute-start(bf16[256,640]{1,0:T(8,128)(2,1)S(1)} %collective-permute-done.5.refs_6_), channel_id=1, source_target_pairs={{0,7},{1,0},{2,1},{3,2},{4,3},{5,4},{6,5},{7,6},{8,15},{9,8},{10,9... | collective-permute-start | bytes 983048 | tf_op jit(solution)/shard_map/ppermute | solution.py:168
  87.2 18.9 %collective-permute-start.2 = (bf16[256,896]{1,0:T(8,128)(2,1)S(1)}, bf16[256,896]{1,0:T(8,128)(2,1)S(1)}, u32[]{:S(2)}, u32[]{:S(2)}) collective-permute-start(bf16[256,896]{1,0:T(8,128)(2,1)S(1)} %slice.69), channel_id=1, source_target_pairs={{0,8},{8,16},{16,24},{24,0},{1,9},{9,17},{17,25},{25,1},{2,10},{10... | collective-permute-start | bytes 1376264 | tf_op jit(solution)/shard_map/ppermute | solution.py:171
  93.4 12.7 %collective-permute-start.3 = (bf16[256,896]{1,0:T(8,128)(2,1)S(1)}, bf16[256,896]{1,0:T(8,128)(2,1)S(1)}, u32[]{:S(2)}, u32[]{:S(2)}) collective-permute-start(bf16[256,896]{1,0:T(8,128)(2,1)S(1)} %slice.70), channel_id=1, source_target_pairs={{0,24},{8,0},{16,8},{24,16},{1,25},{9,1},{17,9},{25,17},{2,26},{10... | collective-permute-start | bytes 1376264 | tf_op jit(solution)/shard_map/ppermute | solution.py:171
  94.7 6.3 %collective-permute-start.10 = (bf16[128,640]{1,0:T(8,128)(2,1)S(1)}, bf16[128,640]{1,0:T(8,128)(2,1)S(1)}, u32[]{:S(2)}, u32[]{:S(2)}) collective-permute-start(bf16[128,640]{1,0:T(8,128)(2,1)S(1)} %slice.72), channel_id=1, source_target_pairs={{0,1},{1,2},{2,3},{3,4},{4,5},{5,6},{6,7},{7,0},{8,9},{9,10},{10,1... | collective-permute-start | bytes 491528 | tf_op jit(solution)/shard_map/ppermute | solution.py:171
  101.0 5.0 %collective-permute-start.11 = (bf16[128,640]{1,0:T(8,128)(2,1)S(1)}, bf16[128,640]{1,0:T(8,128)(2,1)S(1)}, u32[]{:S(2)}, u32[]{:S(2)}) collective-permute-start(bf16[128,640]{1,0:T(8,128)(2,1)S(1)} %slice.73), channel_id=1, source_target_pairs={{0,7},{1,0},{2,1},{3,2},{4,3},{5,4},{6,5},{7,6},{8,15},{9,8},{10,9... | collective-permute-start | bytes 491528 | tf_op jit(solution)/shard_map/ppermute | solution.py:171
  113.8 15.7 %collective-permute-start.15 = (f32[4,256,384]{2,1,0:T(8,128)S(1)}, f32[4,256,384]{2,1,0:T(8,128)S(1)}, u32[]{:S(2)}, u32[]{:S(2)}) collective-permute-start(f32[4,256,384]{2,1,0:T(8,128)S(1)} %get-tuple-element.12), channel_id=1, source_target_pairs={{0,32},{32,0},{64,96},{96,64},{128,160},{160,128},{192,224},{224,1... | collective-permute-start | bytes 4718600 | tf_op jit(solution)/shard_map/ppermute | solution.py:236
  129.8 11.6 %collective-permute-start.16 = (f32[256,384]{1,0:T(8,128)S(1)}, f32[256,384]{1,0:T(8,128)S(1)}, u32[]{:S(2)}, u32[]{:S(2)}) collective-permute-start(f32[256,384]{1,0:T(8,128)S(1)} %pad_maximum_fusion.1), channel_id=1, source_target_pairs={{0,64},{32,96},{64,128},{96,160},{128,192},{160,224},{192,0},{224,... | collective-permute-start | bytes 1179656 | tf_op jit(solution)/shard_map/ppermute | solution.py:238
  130.2 11.2 %collective-permute-start.18 = (f32[256,384]{1,0:T(8,128)S(1)}, f32[256,384]{1,0:T(8,128)S(1)}, u32[]{:S(2)}, u32[]{:S(2)}) collective-permute-start(f32[256,384]{1,0:T(8,128)S(1)} %pad_maximum_fusion.2), channel_id=1, source_target_pairs={{0,192},{32,224},{64,0},{96,32},{128,64},{160,96},{192,128},{224,1... | collective-permute-start | bytes 1179656 | tf_op jit(solution)/shard_map/ppermute | solution.py:239
  141.5 6.5 %collective-permute-start.17 = (f32[128,384]{1,0:T(8,128)S(1)}, f32[128,384]{1,0:T(8,128)S(1)}, u32[]{:S(2)}, u32[]{:S(2)}) collective-permute-start(f32[128,384]{1,0:T(8,128)S(1)} %get-tuple-element.14), channel_id=1, source_target_pairs={{0,64},{32,96},{64,128},{96,160},{128,192},{160,224},{192,0},{224,... | collective-permute-start | bytes 589832 | tf_op jit(solution)/shard_map/ppermute | solution.py:240
  141.6 6.4 %collective-permute-start.19 = (f32[128,384]{1,0:T(8,128)S(1)}, f32[128,384]{1,0:T(8,128)S(1)}, u32[]{:S(2)}, u32[]{:S(2)}) collective-permute-start(f32[128,384]{1,0:T(8,128)S(1)} %get-tuple-element.13), channel_id=1, source_target_pairs={{0,192},{32,224},{64,0},{96,32},{128,64},{160,96},{192,128},{224,1... | collective-permute-start | bytes 589832 | tf_op jit(solution)/shard_map/ppermute | solution.py:241
where the time goes:
time: 150 us; the launch traced here: 149 us
  blocking collectives  61 us (41%)
  starting transfers between devices  39.8 us (27%)
  waiting for transfers between devices  33.7 us (22%)
  Pallas kernels  12.6 us (8%)
    all_gather x1, blocking collectives, body(): z_line = lax.all_gather(piece[:, :split], 'col', axis=0, tiled=True)  26.3 us
    all_to_all x1, blocking collectives, body(): lax.all_to_all(amplitudes[0].reshape(groups, rows // groups, cap), 'grp',...  14.8 us
    ppermute x1, starting transfers between devices, body(): p = keep + lax.ppermute(send, 'grp', swap)  12.6 us
    ppermute x8, starting transfers between devices, ring(): a, b = (lax.ppermute(a, axis, up), lax.ppermute(b, axis, down))  11.8 us
    all_gather x1, blocking collectives, body(): y_line = lax.all_gather(piece[:, split:], 'row', axis=0, tiled=True)  10 us
    all_to_all x1, blocking collectives, body(): piece = lax.all_to_all(packed, 'grp', 0, 0, tiled=True).reshape(rows, wide)  9.92 us
    ppermute x4, waiting for transfers between devices, ring(): ta, tb = (lax.ppermute(a[:h], axis, up), lax.ppermute(b[h:], axis, down))  9.65 us
    ppermute x1, waiting for transfers between devices, body(): a = lax.ppermute(jnp.concatenate([p[2, :h], p[1, h:]]), 'grp', up)  8.76 us
  transfers between devices with their start and end apart: 20, of which 8 were waited for; matrix products, arithmetic and copies ran while one was open for 0% of the time, Pallas kernels for 3%

commit v1 on v0

--- a/solution.py
+++ b/solution.py
@@ -71,8 +71,12 @@
 def pack_amplitudes(groups, own, tiles_ref, assign_ref, src_ref, out_ref, held_ref, block_ref):
     held, total, right, left = balance(tiles_ref, assign_ref, held_ref, block_ref, groups)
     blocks = [block_ref[s] for s in range(groups)]
+    group = lax.axis_index("grp")
+    x, core = lax.div(group, 2), lax.rem(group, 2)
+    chips = groups // 2
     for g in range(groups):
-        place = 0
+        place = lax.rem(g // 2 - x + chips, chips) * own
+        side = jnp.where(core == g % 2, 0, 1)
         for chip, start, count in plan(g // 2, g % 2, total, right, left, own):
             n0 = jnp.clip(held[2 * chip] - start, 0, count)
             second = jnp.maximum(start - held[2 * chip], 0)
@@ -80,7 +84,7 @@
 
                 def move(i, carry, block=block, tile=tile, place=place):
                     into = pl.ds(pl.multiple_of((place + i) * TP, TP), TP)
-                    out_ref[g, :, into] = src_ref[block, :, pl.ds(pl.multiple_of((tile + i) * TP, TP), TP)]
+                    out_ref[side, :, into] = src_ref[block, :, pl.ds(pl.multiple_of((tile + i) * TP, TP), TP)]
                     return carry
 
                 lax.fori_loop(0, many, move, 0)
@@ -131,37 +135,50 @@
     copy_run(border, core, start, count, mine_ref, other_ref, out_ref, nl + nr)
 
 
-def multiply(ny, nz, rows, *refs):
-    zs, ys, (b_ref, keep_ref, send_ref) = refs[:ny], refs[ny : ny + nz], refs[ny + nz :]
+def multiply(ny, nz, *refs):
+    zs, ys, (b0, b1, b2, b3, b4, out_ref, za_ref, ya_ref) = refs[:ny], refs[ny : ny + nz], refs[ny + nz :]
     group, y, z = lax.axis_index("grp"), lax.axis_index("row"), lax.axis_index("col")
-    x, core = lax.div(group, 2), lax.rem(group, 2)
-    wide = zs[0].shape[1]
-    part = rows * nz // 2
+    core = lax.rem(group, 2)
+    zrows, zwide = zs[0].shape
+    yrows = ys[0].shape[0]
+    rows = yrows // ny
     for r in range(ny):
-        d = lax.rem(y + r - x + ny, ny)
-        out = jnp.dot(zs[r][...], b_ref[:wide, :], preferred_element_type=jnp.float32)
-        keep_ref[d] = jnp.where(core == 0, out[:part], out[part:])
-        send_ref[d] = jnp.where(core == 0, out[part:], out[:part])
+        za_ref[r * zrows : (r + 1) * zrows, :] = zs[r][...]
     for r in range(nz):
-        at = lax.rem(z + r, nz)
-        side = lax.div(at, nz // 2)
-        into = pl.ds(pl.multiple_of(lax.rem(at, nz // 2) * rows, rows), rows)
-        out = jnp.dot(ys[r][...], b_ref[wide:, :], preferred_element_type=jnp.float32)
-        for ref, here in ((keep_ref, side == core), (send_ref, side != core)):
-
-            @pl.when(here)
-            def _(ref=ref, out=out):
-                for q in range(ny):
-                    d = lax.rem(q - x + ny, ny)
-                    ref[d, into, :] += out[q * rows : (q + 1) * rows]
+        ya_ref[r * yrows : (r + 1) * yrows, :] = ys[r][...]
+
+    def runs(a_ref, parts):
+        at, out = 0, None
+        for part in parts:
+            term = jnp.dot(a_ref[:, at : at + part.shape[0]], part[...], preferred_element_type=jnp.float32)
+            out = term if out is None else out + term
+            at += part.shape[0]
+        return out
+
+    cut = zwide - b0.shape[0] - b1.shape[0]
+    out = runs(za_ref, (b0, b1, b2.at[:cut]))
+    for r in range(ny):
+        at_y = lax.rem(y + r, ny)
+        for q in range(nz):
+            at = lax.rem(z + q, nz)
+            side = jnp.where(lax.div(at, nz // 2) == core, 0, 1)
+            first = r * zrows + q * rows
+            out_ref[side, at_y, lax.rem(at, nz // 2)] = out[first : first + rows]
+    out = runs(ya_ref, (b2.at[cut:], b3, b4))
+    for q in range(nz):
+        at = lax.rem(z + q, nz)
+        side = jnp.where(lax.div(at, nz // 2) == core, 0, 1)
+        for r in range(ny):
+            first = q * yrows + r * rows
+            out_ref[side, r, lax.rem(at, nz // 2)] += out[first : first + rows]
 
 
 def steps(n):
     return [(i, (i + 1) % n) for i in range(n)], [(i, (i - 1) % n) for i in range(n)]
 
 
-def ring(block, axis, n):
-    up, down = steps(n)
+def ring(block, axis, up, down, half_way):
+    n = len(up) if axis != "grp" else len(up) // 2
     out = [block] * n
     a = b = block
     for s in range(1, n // 2):
@@ -169,35 +186,37 @@
         out[n - s], out[s] = a, b
     h = block.shape[0] // 2
     ta, tb = lax.ppermute(a[:h], axis, up), lax.ppermute(b[h:], axis, down)
-    out[n // 2] = jnp.concatenate([ta, tb], axis=0)
+    out[n // 2] = (ta, tb) if half_way else jnp.concatenate([ta, tb], axis=0)
     return out
 
 
 def body(amplitudes, integrals, block_tiles, assign):
     groups = assign.shape[0]
+    chips = groups // 2
     _, rows, cap = amplitudes.shape
     cols = integrals.shape[2]
     ny, nz = lax.axis_size("row"), lax.axis_size("col")
     own = 12
     wide = own * TP
-    split = 7 * TP
+    split = 28 * TP
+    octet = rows // groups
     small = [pltpu.SMEM((groups,), jnp.int32)] * 2
     swap = [(g, g ^ 1) for g in range(groups)]
     up = [(g, (g + 2) % groups) for g in range(groups)]
     down = [(g, (g - 2) % groups) for g in range(groups)]
     limit = pltpu.CompilerParams(vmem_limit_bytes=24 * 2**20)
+    core = lax.rem(lax.axis_index("grp"), 2)
 
     mine = integrals[0]
     other = lax.ppermute(mine, "grp", swap)
-    moved = lax.all_to_all(amplitudes[0].reshape(groups, rows // groups, cap), "grp", 0, 0, tiled=True)
+    moved = lax.all_to_all(amplitudes[0].reshape(groups, octet, cap), "grp", 0, 0, tiled=True)
     packed = pl.pallas_call(
         functools.partial(pack_amplitudes, groups, own),
-        out_shape=jax.ShapeDtypeStruct((groups, rows // groups, wide), jnp.bfloat16),
+        out_shape=jax.ShapeDtypeStruct((2, octet, chips * wide), jnp.bfloat16),
         in_specs=[SMEM, SMEM, VMEM],
         out_specs=VMEM,
         scratch_shapes=small,
     )(block_tiles, assign, moved)
-    piece = lax.all_to_all(packed, "grp", 0, 0, tiled=True).reshape(rows, wide)
 
     sends = jax.ShapeDtypeStruct((wide, cols), jnp.bfloat16)
     to_right, to_left = pl.pallas_call(
@@ -208,8 +227,15 @@
         scratch_shapes=small,
         compiler_params=limit,
     )(block_tiles, assign, mine, other)
+    packed, to_right, to_left = lax.optimization_barrier((packed, to_right, to_left))
     from_left = lax.ppermute(to_right, "grp", up)
     from_right = lax.ppermute(to_left, "grp", down)
+
+    theirs = lax.ppermute(packed[1], "grp", swap)
+    piece = jnp.where(core == 0, jnp.concatenate([packed[0], theirs]), jnp.concatenate([theirs, packed[0]]))
+    y_line = lax.all_gather(piece[:, split:], "row", axis=0, tiled=True)
+    z_line = jnp.concatenate(ring(piece[:, :split], "col", *steps(nz), False))
+
     held = pl.pallas_call(
         functools.partial(join_tiles, groups, own),
         out_shape=sends,
@@ -218,28 +244,27 @@
         scratch_shapes=small,
         compiler_params=limit,
     )(block_tiles, assign, mine, other, from_left, from_right)
-
-    y_line = lax.all_gather(piece[:, split:], "row", axis=0, tiled=True)
-    z_line = lax.all_gather(piece[:, :split], "col", axis=0, tiled=True)
-    zs = ring(z_line, "row", ny)
-    ys = ring(y_line, "col", nz)
-    half_rows = rows * nz // 2
-    kept = jax.ShapeDtypeStruct((ny, half_rows, cols), jnp.float32)
-    keep, send = pl.pallas_call(
-        functools.partial(multiply, ny, nz, rows),
-        out_shape=(kept, kept),
-        in_specs=[VMEM] * (ny + nz + 1),
-        out_specs=(VMEM, VMEM),
-        compiler_params=pltpu.CompilerParams(vmem_limit_bytes=32 * 2**20),
-    )(*zs, *ys, held)
-
-    p = keep + lax.ppermute(send, "grp", swap)
-    h = half_rows // 2
-    a = lax.ppermute(jnp.concatenate([p[2, :h], p[1, h:]]), "grp", up)
-    b = lax.ppermute(jnp.concatenate([p[2, h:], p[3, :h]]), "grp", down)
-    a2 = lax.ppermute(p[1, :h] + a[:h], "grp", up)
-    b2 = lax.ppermute(p[3, h:] + b[:h], "grp", down)
-    return p[0] + jnp.concatenate([a2, a[h:]]) + jnp.concatenate([b[h:], b2])
+    y_line, z_line, held = lax.optimization_barrier((y_line, z_line, held))
+
+    zs = ring(z_line, "row", *steps(ny), False)
+    ys = ring(y_line, "col", *steps(nz), False)
+    b0, b1, (b2, b3), b4 = ring(held, "grp", up, down, True)
+    sums = pl.pallas_call(
+        functools.partial(multiply, ny, nz),
+        out_shape=jax.ShapeDtypeStruct((2, ny, nz // 2, 2 * octet, cols), jnp.float32),
+        in_specs=[VMEM] * (ny + nz + 5),
+        out_specs=VMEM,
+        scratch_shapes=[
+            pltpu.VMEM((2 * octet * ny * nz, split), jnp.bfloat16),
+            pltpu.VMEM((2 * octet * ny * nz, chips * wide - split), jnp.bfloat16),
+        ],
+        compiler_params=pltpu.CompilerParams(vmem_limit_bytes=40 * 2**20),
+    )(*zs, *ys, b0, b1, b2, b3, b4)
+
+    done = sums[0] + lax.ppermute(sums[1], "grp", swap)
+    lines = [[2 * x + c for x in range(chips)] for c in range(2)]
+    got = lax.all_to_all(done, "grp", 0, 0, axis_index_groups=lines, tiled=True)
+    return got.transpose(1, 0, 2, 3).reshape(nz // 2 * chips * 2 * octet, cols)
 
 
 def solution(mesh):

time: 150 us -> 149 us (level)
  blocking collectives: 61 us -> 37.5 us
  starting transfers between devices: 39.8 us -> 59.3 us
  local copies, waits for them, and re-layouts: 0.19 us -> 8.2 us
  Pallas kernels: 12.6 us -> 7.9 us
    all_gather x1 -> x0, blocking collectives: 26.3 us -> none  [body(): z_line = lax.all_gather(piece[:, :split], 'col', axis=0, tiled=True)]
    ppermute x8 -> x16, waiting for transfers between devices: 8.56 us -> 23.7 us  [ring(): a, b = (lax.ppermute(a, axis, up), lax.ppermute(b, axis, down))]
    ppermute x5 -> x2, waiting for transfers between devices: 15.5 us -> 1.35 us  [the longest x1 1.35 us: body(): done = sums[0] + lax.ppermute(sums[1], 'grp', swap)]
    ppermute x8 -> x16, starting transfers between devices: 11.8 us -> 24.3 us  [ring(): a, b = (lax.ppermute(a, axis, up), lax.ppermute(b, axis, down))]
    ppermute x4 -> x8, starting transfers between devices: 3.72 us -> 11.6 us  [ring(): ta, tb = (lax.ppermute(a[:h], axis, up), lax.ppermute(b[h:], axis, down))]
    unnamed x6 -> x25, local copies, waits for them, and re-layouts: 0.01 us -> 6.47 us
    pallas_call x1, Pallas kernels: 5.29 us -> 3.42 us  [body(): pl.pallas_call(functools.partial(multiply, ny, nz), out_shape=jax.ShapeDt...]
    all_to_all x2, blocking collectives: 24.7 us -> 26.3 us  [the longest x1 14.7 us: body(): lax.all_to_all(amplitudes[0].reshape(groups, octet, cap), 'grp', 0, 0, ti...]
  transfers between devices with their start and end apart: 20 -> 29, of which waited for: 8 -> 12; matrix products, arithmetic and copies ran while one was open for 0% -> 1% of each run, Pallas kernels for 3% -> 2%
where the time goes in v1:
time: 149 us
  starting transfers between devices  59.3 us (40%)
  blocking collectives  37.5 us (25%)
  waiting for transfers between devices  34.2 us (23%)
  local copies, waits for them, and re-layouts  8.2 us (6%)
  Pallas kernels  7.9 us (5%)
    ppermute x16, starting transfers between devices, ring(): a, b = (lax.ppermute(a, axis, up), lax.ppermute(b, axis, down))  24.3 us
    ppermute x16, waiting for transfers between devices, ring(): a, b = (lax.ppermute(a, axis, up), lax.ppermute(b, axis, down))  23.7 us
    ppermute x1, starting transfers between devices, body(): done = sums[0] + lax.ppermute(sums[1], 'grp', swap)  16.7 us
    all_to_all x1, blocking collectives, body(): lax.all_to_all(amplitudes[0].reshape(groups, octet, cap), 'grp', 0, 0, ti...  14.7 us
    ppermute x8, starting transfers between devices, ring(): ta, tb = (lax.ppermute(a[:h], axis, up), lax.ppermute(b[h:], axis, down))  11.6 us
    all_to_all x1, blocking collectives, body(): got = lax.all_to_all(done, 'grp', 0, 0, axis_index_groups=lines, tiled=True)  11.6 us
    all_gather x1, blocking collectives, body(): y_line = lax.all_gather(piece[:, split:], 'row', axis=0, tiled=True)  11.3 us
    ppermute x8, waiting for transfers between devices, ring(): ta, tb = (lax.ppermute(a[:h], axis, up), lax.ppermute(b[h:], axis, down))  9.06 us
  transfers between devices with their start and end apart: 29, of which 12 were waited for; matrix products, arithmetic and copies ran while one was open for 1% of the time, Pallas kernels for 2%

profile of v1, /device:TPU:1, one launch (start us, length us, event | category | flops | bytes accessed | tf_op | source)
XLA Modules:
  0.0 148.5 jit_solution(12872321700233069721)
XLA Ops:
  0.0 3.2 %collective-permute-start = (bf16[4608,384]{1,0:T(8,128)(2,1)}, bf16[4608,384]{1,0:T(8,128)(2,1)S(1)}, u32[]{:S(2)}, u32[]{:S(2)}) collective-permute-start(bf16[4608,384]{1,0:T(8,128)(2,1)} %bitcast.14), channel_id=1, source_target_pairs={{0,32},{32,0},{64,96},{96,64},{128,160},{160,128},{192,224},{224,1... | collective-permute-start | bytes 10616840 | tf_op jit(solution)/shard_map/ppermute | solution.py:211
  3.2 14.7 %all_to_all.10.src_ref = bf16[8,8,4608]{2,1,0:T(8,128)(2,1)} all-to-all(bf16[8,8,4608]{2,1,0:T(8,128)(2,1)} %bitcast.18), channel_id=1, replica_groups=mesh['grp'=8,'row'=4,'col'=8] {'grp'}, dimensions={0} | all-to-all | bytes 1179648 | tf_op jit(solution)/shard_map/all_to_all | solution.py:212
  17.9 2.9 %shard_map.46 = bf16[2,8,6144]{2,1,0:T(8,128)(2,1)} custom-call(s32[8]{0:T(128)} %tiles_ref.5, s32[8]{0:T(128)} %assign_ref.5, bf16[8,8,4608]{2,1,0:T(8,128)(2,1)} %all_to_all.10.src_ref), custom_call_target="tpu_custom_call" | custom-call | tf_op jit(solution)/shard_map/pallas_call | solution.py:213
  20.8 0.0 collective-permute-done.other_ref
  20.8 0.0 copy-start
  20.9 2.0 %copy-done = bf16[1,4608,384]{2,1,0:T(8,128)(2,1)S(1)} copy-done((bf16[1,4608,384]{2,1,0:T(8,128)(2,1)S(1)}, bf16[1,4608,384]{2,1,0:T(8,128)(2,1)}, u32[]{:S(2)}) %copy-start) | copy-done | bytes 3538968
  22.9 0.8 shard_map.47
  23.6 1.0 copy-done.2
  24.6 1.0 copy-done.6
  25.6 0.4 copy-done.7
  26.0 0.7 slice_bitcast_fusion.3
  26.7 0.7 collective-permute-start.1
  27.5 0.3 collective-permute-start.10
  27.7 2.4 %collective-permute-start.11 = (bf16[1536,384]{1,0:T(8,128)(2,1)}, bf16[1536,384]{1,0:T(8,128)(2,1)S(1)}, u32[]{:S(2)}, u32[]{:S(2)}) collective-permute-start(bf16[1536,384]{1,0:T(8,128)(2,1)} %copy-done.6), channel_id=1, source_target_pairs={{0,192},{32,224},{64,0},{96,32},{128,64},{160,96},{192,128},{224,1... | collective-permute-start | bytes 3538952 | tf_op jit(solution)/shard_map/ppermute | solution.py:232
  30.1 1.1 maximum_select_fusion
  31.3 0.2 collective-permute-start.5
  31.5 4.0 %collective-permute-start.2 = (bf16[16,3584]{1,0:T(8,128)(2,1)S(1)}, bf16[16,3584]{1,0:T(8,128)(2,1)S(1)}, u32[]{:S(2)}, u32[]{:S(2)}) collective-permute-start(bf16[16,3584]{1,0:T(8,128)(2,1)S(1)} %get-tuple-element.21), channel_id=1, source_target_pairs={{0,7},{1,0},{2,1},{3,2},{4,3},{5,4},{6,5},{7,6},{8,15},{9,8},{10,9... | collective-permute-start | bytes 344072 | tf_op jit(solution)/shard_map/ppermute | solution.py:185
  35.5 11.3 %all_gather.3.refs_4_ = bf16[64,2560]{1,0:T(8,128)(2,1)S(1)} all-gather(bf16[16,2560]{1,0:T(8,128)(2,1)S(1)} %slice.57), channel_id=1, replica_groups=mesh['grp'=8,'row'=4,'col'=8] {'row'}, dimensions={0}, use_global_device_ids=true | all-gather | bytes 409600 | tf_op jit(solution)/shard_map/all_gather | solution.py:236
  46.8 0.0 collective-permute-done.5
  46.8 0.0 collective-permute-start.6
  46.8 0.0 collective-permute-done.2
  46.8 2.7 %collective-permute-start.3 = (bf16[16,3584]{1,0:T(8,128)(2,1)S(1)}, bf16[16,3584]{1,0:T(8,128)(2,1)S(1)}, u32[]{:S(2)}, u32[]{:S(2)}) collective-permute-start(bf16[16,3584]{1,0:T(8,128)(2,1)S(1)} %collective-permute-done.2), channel_id=1, source_target_pairs={{0,7},{1,0},{2,1},{3,2},{4,3},{5,4},{6,5},{7,6},{8,15},{9,8},{10,9... | collective-permute-start | bytes 344072 | tf_op jit(solution)/shard_map/ppermute | solution.py:185
  49.5 2.5 %collective-permute-done.6 = bf16[16,3584]{1,0:T(8,128)(2,1)S(1)} collective-permute-done((bf16[16,3584]{1,0:T(8,128)(2,1)S(1)}, bf16[16,3584]{1,0:T(8,128)(2,1)S(1)}, u32[]{:S(2)}, u32[]{:S(2)}) %collective-permute-start.6) | collective-permute-done | bytes 114720 | tf_op jit(solution)/shard_map/ppermute | solution.py:185
  51.9 0.0 collective-permute-start.7
  51.9 0.0 collective-permute-done.3
  51.9 2.7 %collective-permute-start.4 = (bf16[16,3584]{1,0:T(8,128)(2,1)S(1)}, bf16[16,3584]{1,0:T(8,128)(2,1)S(1)}, u32[]{:S(2)}, u32[]{:S(2)}) collective-permute-start(bf16[16,3584]{1,0:T(8,128)(2,1)S(1)} %collective-permute-done.3), channel_id=1, source_target_pairs={{0,7},{1,0},{2,1},{3,2},{4,3},{5,4},{6,5},{7,6},{8,15},{9,8},{10,9... | collective-permute-start | bytes 344072 | tf_op jit(solution)/shard_map/ppermute | solution.py:185
  54.6 2.2 %collective-permute-done.7 = bf16[16,3584]{1,0:T(8,128)(2,1)S(1)} collective-permute-done((bf16[16,3584]{1,0:T(8,128)(2,1)S(1)}, bf16[16,3584]{1,0:T(8,128)(2,1)S(1)}, u32[]{:S(2)}, u32[]{:S(2)}) %collective-permute-start.7) | collective-permute-done | bytes 114720 | tf_op jit(solution)/shard_map/ppermute | solution.py:185
  56.9 0.0 collective-permute-done.4
  56.9 2.9 %collective-permute-start.9 = (bf16[8,3584]{1,0:T(8,128)(2,1)S(1)}, bf16[8,3584]{1,0:T(8,128)(2,1)S(1)}, u32[]{:S(2)}, u32[]{:S(2)}) collective-permute-start(bf16[8,3584]{1,0:T(8,128)(2,1)S(1)} %slice.60), channel_id=1, source_target_pairs={{0,7},{1,0},{2,1},{3,2},{4,3},{5,4},{6,5},{7,6},{8,15},{9,8},{10,9... | collective-permute-start | bytes 172040 | tf_op jit(solution)/shard_map/ppermute | solution.py:188
  59.8 1.4 collective-permute-done.8
  61.2 0.0 collective-permute-done.9
  61.3 2.0 %copy-done.3 = bf16[4608,384]{1,0:T(8,128)(2,1)S(1)} copy-done((bf16[4608,384]{1,0:T(8,128)(2,1)S(1)}, bf16[4608,384]{1,0:T(8,128)(2,1)}, u32[]{:S(2)}) %copy-start.3) | copy-done | bytes 3538968
  63.3 0.8 shard_map.48.refs_12_
  64.1 0.1 collective-permute-start.19
  64.2 3.0 %collective-permute-start.16 = (bf16[64,2560]{1,0:T(8,128)(2,1)S(1)}, bf16[64,2560]{1,0:T(8,128)(2,1)S(1)}, u32[]{:S(2)}, u32[]{:S(2)}) collective-permute-start(bf16[64,2560]{1,0:T(8,128)(2,1)S(1)} %all_gather.3.refs_4_), channel_id=1, source_target_pairs={{0,7},{1,0},{2,1},{3,2},{4,3},{5,4},{6,5},{7,6},{8,15},{9,8},{10,9... | collective-permute-start | bytes 983048 | tf_op jit(solution)/shard_map/ppermute | solution.py:185
  67.2 4.4 %collective-permute-done.19.refs_11_ = bf16[64,2560]{1,0:T(8,128)(2,1)S(1)} collective-permute-done((bf16[64,2560]{1,0:T(8,128)(2,1)S(1)}, bf16[64,2560]{1,0:T(8,128)(2,1)S(1)}, u32[]{:S(2)}, u32[]{:S(2)}) %collective-permute-start.19) | collective-permute-done | bytes 327712 | tf_op jit(solution)/shard_map/ppermute | solution.py:185
  71.6 0.0 collective-permute-start.20
  71.6 2.7 %collective-permute-start.24 = (bf16[1536,384]{1,0:T(8,128)(2,1)S(1)}, bf16[1536,384]{1,0:T(8,128)(2,1)S(1)}, u32[]{:S(2)}, u32[]{:S(2)}) collective-permute-start(bf16[1536,384]{1,0:T(8,128)(2,1)S(1)} %shard_map.48.refs_12_), channel_id=1, source_target_pairs={{0,192},{32,224},{64,0},{96,32},{128,64},{160,96},{192,128},{224,1... | collective-permute-start | bytes 3538952 | tf_op jit(solution)/shard_map/ppermute | solution.py:185
  74.3 2.7 %collective-permute-start.17 = (bf16[64,2560]{1,0:T(8,128)(2,1)S(1)}, bf16[64,2560]{1,0:T(8,128)(2,1)S(1)}, u32[]{:S(2)}, u32[]{:S(2)}) collective-permute-start(bf16[64,2560]{1,0:T(8,128)(2,1)S(1)} %collective-permute-done.16.refs_5_), channel_id=1, source_target_pairs={{0,7},{1,0},{2,1},{3,2},{4,3},{5,4},{6,5},{7,6},{8,15},{9,8},{10,9... | collective-permute-start | bytes 983048 | tf_op jit(solution)/shard_map/ppermute | solution.py:185
  76.9 1.3 collective-permute-start.13
  78.3 2.6 %collective-permute-done.20.refs_10_ = bf16[64,2560]{1,0:T(8,128)(2,1)S(1)} collective-permute-done((bf16[64,2560]{1,0:T(8,128)(2,1)S(1)}, bf16[64,2560]{1,0:T(8,128)(2,1)S(1)}, u32[]{:S(2)}, u32[]{:S(2)}) %collective-permute-start.20) | collective-permute-done | bytes 327712 | tf_op jit(solution)/shard_map/ppermute | solution.py:185
  80.9 3.2 %collective-permute-start.12 = (bf16[128,3584]{1,0:T(8,128)(2,1)S(1)}, bf16[128,3584]{1,0:T(8,128)(2,1)S(1)}, u32[]{:S(2)}, u32[]{:S(2)}) collective-permute-start(bf16[128,3584]{1,0:T(8,128)(2,1)S(1)} %constant_dynamic-update-slice_fusion.refs_0_), channel_id=1, source_target_pairs={{0,24},{8,0},{16,8},{24,16},{1,25},{9,1},{17,9},{25,17},{2,26},{10... | collective-permute-start | bytes 2752520 | tf_op jit(solution)/shard_map/ppermute | solution.py:185
  84.0 7.6 %collective-permute-done.21.refs_9_ = bf16[64,2560]{1,0:T(8,128)(2,1)S(1)} collective-permute-done((bf16[64,2560]{1,0:T(8,128)(2,1)S(1)}, bf16[64,2560]{1,0:T(8,128)(2,1)S(1)}, u32[]{:S(2)}, u32[]{:S(2)}) %collective-permute-start.21) | collective-permute-done | bytes 327712 | tf_op jit(solution)/shard_map/ppermute | solution.py:185
  91.6 1.7 %collective-permute-start.18 = (bf16[64,2560]{1,0:T(8,128)(2,1)S(1)}, bf16[64,2560]{1,0:T(8,128)(2,1)S(1)}, u32[]{:S(2)}, u32[]{:S(2)}) collective-permute-start(bf16[64,2560]{1,0:T(8,128)(2,1)S(1)} %collective-permute-done.17.refs_6_), channel_id=1, source_target_pairs={{0,7},{1,0},{2,1},{3,2},{4,3},{5,4},{6,5},{7,6},{8,15},{9,8},{10,9... | collective-permute-start | bytes 983048 | tf_op jit(solution)/shard_map/ppermute | solution.py:185
  93.4 4.5 %collective-permute-done.18.refs_7_ = bf16[64,2560]{1,0:T(8,128)(2,1)S(1)} collective-permute-done((bf16[64,2560]{1,0:T(8,128)(2,1)S(1)}, bf16[64,2560]{1,0:T(8,128)(2,1)S(1)}, u32[]{:S(2)}, u32[]{:S(2)}) %collective-permute-start.18) | collective-permute-done | bytes 327712 | tf_op jit(solution)/shard_map/ppermute | solution.py:185
  97.8 0.5 collective-permute-start.22
  98.3 2.6 %collective-permute-start.23 = (bf16[32,2560]{1,0:T(8,128)(2,1)S(1)}, bf16[32,2560]{1,0:T(8,128)(2,1)S(1)}, u32[]{:S(2)}, u32[]{:S(2)}) collective-permute-start(bf16[32,2560]{1,0:T(8,128)(2,1)S(1)} %slice.64), channel_id=1, source_target_pairs={{0,7},{1,0},{2,1},{3,2},{4,3},{5,4},{6,5},{7,6},{8,15},{9,8},{10,9... | collective-permute-start | bytes 491528 | tf_op jit(solution)/shard_map/ppermute | solution.py:188
  100.9 2.2 %collective-permute-start.14 = (bf16[64,3584]{1,0:T(8,128)(2,1)S(1)}, bf16[64,3584]{1,0:T(8,128)(2,1)S(1)}, u32[]{:S(2)}, u32[]{:S(2)}) collective-permute-start(bf16[64,3584]{1,0:T(8,128)(2,1)S(1)} %slice.61), channel_id=1, source_target_pairs={{0,8},{8,16},{16,24},{24,0},{1,9},{9,17},{17,25},{25,1},{2,10},{10... | collective-permute-start | bytes 1376264 | tf_op jit(solution)/shard_map/ppermute | solution.py:188
  103.2 1.3 collective-permute-start.15
  104.5 0.1 slice.65
  104.6 0.1 collective-permute-start.26
  104.7 0.1 slice.66
  104.8 0.8 collective-permute-done.22
  105.6 2.1 %collective-permute-start.27 = (bf16[768,384]{1,0:T(8,128)(2,1)S(1)}, bf16[768,384]{1,0:T(8,128)(2,1)S(1)}, u32[]{:S(2)}, u32[]{:S(2)}) collective-permute-start(bf16[768,384]{1,0:T(8,128)(2,1)S(1)} %slice.66), channel_id=1, source_target_pairs={{0,192},{32,224},{64,0},{96,32},{128,64},{160,96},{192,128},{224,1... | collective-permute-start | bytes 1769480 | tf_op jit(solution)/shard_map/ppermute | solution.py:188
  107.8 2.5 %collective-permute-done.14 = bf16[64,3584]{1,0:T(8,128)(2,1)S(1)} collective-permute-done((bf16[64,3584]{1,0:T(8,128)(2,1)S(1)}, bf16[64,3584]{1,0:T(8,128)(2,1)S(1)}, u32[]{:S(2)}, u32[]{:S(2)}) %collective-permute-start.14) | collective-permute-done | bytes 458784 | tf_op jit(solution)/shard_map/ppermute | solution.py:188
  110.3 1.2 collective-permute-done.15
  111.5 0.1 pad_maximum_fusion.refs_2_
  111.5 3.1 %collective-permute-done.26.refs_14_ = bf16[768,384]{1,0:T(8,128)(2,1)S(1)} collective-permute-done((bf16[768,384]{1,0:T(8,128)(2,1)S(1)}, bf16[768,384]{1,0:T(8,128)(2,1)S(1)}, u32[]{:S(2)}, u32[]{:S(2)}) %collective-permute-start.26) | collective-permute-done | bytes 589856 | tf_op jit(solution)/shard_map/ppermute | solution.py:188
  114.6 3.4 %shard_map.49 = f32[2,4,4,16,384]{4,3,2,1,0:T(8,128)S(1)} custom-call(bf16[128,3584]{1,0:T(8,128)(2,1)S(1)} %constant_dynamic-update-slice_fusion.refs_0_, bf16[128,3584]{1,0:T(8,128)(2,1)S(1)} %collective-permute-done.12.refs_1_, bf16[128,3584]{1,0:T(8,128)(2,1)S(1)} %pad_maximum_fusion.refs_2_, bf16[128,3584]{1,0:T(8,128)(2,1)S(1)} %collective-permute-done.13.refs_3_, ...), custom_call_target="tpu_custom_call" | custom-call | tf_op jit(solution)/shard_map/pallas_call | solution.py:252
  118.1 16.7 %collective-permute-start.28 = (f32[4,4,16,384]{3,2,1,0:T(8,128)S(1)}, f32[4,4,16,384]{3,2,1,0:T(8,128)S(1)}, u32[]{:S(2)}, u32[]{:S(2)}) collective-permute-start(f32[4,4,16,384]{3,2,1,0:T(8,128)S(1)} %slice_bitcast_fusion), channel_id=1, source_target_pairs={{0,32},{32,0},{64,96},{96,64},{128,160},{160,128},{192,224},{224,1... | collective-permute-start | bytes 1179656 | tf_op jit(solution)/shard_map/ppermute | solution.py:264
  134.8 1.3 collective-permute-done.28
  136.1 0.1 fusion
  136.2 11.6 %all_to_all.11 = f32[4,4,16,384]{3,2,1,0:T(8,128)S(1)} all-to-all(f32[4,4,16,384]{3,2,1,0:T(8,128)S(1)} %fusion), channel_id=1, replica_groups={{0,64,128,192},{32,96,160,224},{1,65,129,193},{33,97,161,225},{2,66,130..., dimensions={0} | all-to-all | bytes 786432 | tf_op jit(solution)/shard_map/all_to_all | solution.py:266
  147.8 0.8 copy.5
  (44 shorter events, 0.3 us)
Async XLA Ops:
  0.0 20.8 %copy-start.5 = (s32[8]{0:T(128)S(1)}, s32[8]{0:T(128)}, u32[]{:S(2)}) copy-start(s32[8]{0:T(128)} %assign_ref.5) | copy-start | bytes 100
  0.0 20.8 %copy-start.4 = (s32[8]{0:T(128)S(1)}, s32[8]{0:T(128)}, u32[]{:S(2)}) copy-start(s32[8]{0:T(128)} %tiles_ref.5) | copy-start | bytes 100
  0.0 20.8 %collective-permute-start = (bf16[4608,384]{1,0:T(8,128)(2,1)}, bf16[4608,384]{1,0:T(8,128)(2,1)S(1)}, u32[]{:S(2)}, u32[]{:S(2)}) collective-permute-start(bf16[4608,384]{1,0:T(8,128)(2,1)} %bitcast.14), channel_id=1, source_target_pairs={{0,32},{32,0},{64,96},{96,64},{128,160},{160,128},{192,224},{224,1... | collective-permute-start | bytes 10616840 | tf_op jit(solution)/shard_map/ppermute | solution.py:211
  20.8 2.0 %copy-start = (bf16[1,4608,384]{2,1,0:T(8,128)(2,1)S(1)}, bf16[1,4608,384]{2,1,0:T(8,128)(2,1)}, u32[]{:S(2)}) copy-start(bf16[1,4608,384]{2,1,0:T(8,128)(2,1)} %param.5) | copy-start | bytes 10616836
  22.8 1.7 %copy-start.2 = (bf16[4608,384]{1,0:T(8,128)(2,1)}, bf16[4608,384]{1,0:T(8,128)(2,1)S(1)}, u32[]{:S(2)}) copy-start(bf16[4608,384]{1,0:T(8,128)(2,1)S(1)} %collective-permute-done.other_ref) | copy-start | bytes 10616836
  22.9 3.2 %copy-start.8 = (bf16[2,8,6144]{2,1,0:T(8,128)(2,1)S(1)}, bf16[2,8,6144]{2,1,0:T(8,128)(2,1)}, u32[]{:S(2)}) copy-start(bf16[2,8,6144]{2,1,0:T(8,128)(2,1)} %shard_map.46) | copy-start | bytes 589828
  24.6 1.0 copy-start.6
  24.6 1.4 copy-start.7
  26.0 35.3 %copy-start.1 = (bf16[1,4608,384]{2,1,0:T(8,128)(2,1)S(1)}, bf16[1,4608,384]{2,1,0:T(8,128)(2,1)}, u32[]{:S(2)}) copy-start(bf16[1,4608,384]{2,1,0:T(8,128)(2,1)} %param.5) | copy-start | bytes 10616836
  26.7 3.4 %collective-permute-start.1 = (bf16[8,6144]{1,0:T(8,128)(2,1)}, bf16[8,6144]{1,0:T(8,128)(2,1)}, u32[]{:S(2)}, u32[]{:S(2)}) collective-permute-start(bf16[8,6144]{1,0:T(8,128)(2,1)} %get-tuple-element.24), channel_id=1, source_target_pairs={{0,32},{32,0},{64,96},{96,64},{128,160},{160,128},{192,224},{224,1... | collective-permute-start | bytes 294920 | tf_op jit(solution)/shard_map/ppermute | solution.py:234
  27.5 33.8 %collective-permute-start.10 = (bf16[1536,384]{1,0:T(8,128)(2,1)}, bf16[1536,384]{1,0:T(8,128)(2,1)S(1)}, u32[]{:S(2)}, u32[]{:S(2)}) collective-permute-start(bf16[1536,384]{1,0:T(8,128)(2,1)} %copy-done.7), channel_id=1, source_target_pairs={{0,64},{32,96},{64,128},{96,160},{128,192},{160,224},{192,0},{224,... | collective-permute-start | bytes 3538952 | tf_op jit(solution)/shard_map/ppermute | solution.py:231
  27.7 33.5 %collective-permute-start.11 = (bf16[1536,384]{1,0:T(8,128)(2,1)}, bf16[1536,384]{1,0:T(8,128)(2,1)S(1)}, u32[]{:S(2)}, u32[]{:S(2)}) collective-permute-start(bf16[1536,384]{1,0:T(8,128)(2,1)} %copy-done.6), channel_id=1, source_target_pairs={{0,192},{32,224},{64,0},{96,32},{128,64},{160,96},{192,128},{224,1... | collective-permute-start | bytes 3538952 | tf_op jit(solution)/shard_map/ppermute | solution.py:232
  31.3 15.5 %collective-permute-start.5 = (bf16[16,3584]{1,0:T(8,128)(2,1)S(1)}, bf16[16,3584]{1,0:T(8,128)(2,1)S(1)}, u32[]{:S(2)}, u32[]{:S(2)}) collective-permute-start(bf16[16,3584]{1,0:T(8,128)(2,1)S(1)} %get-tuple-element.21), channel_id=1, source_target_pairs={{0,1},{1,2},{2,3},{3,4},{4,5},{5,6},{6,7},{7,0},{8,9},{9,10},{10,1... | collective-permute-start | bytes 344072 | tf_op jit(solution)/shard_map/ppermute | solution.py:185
  31.5 15.3 %collective-permute-start.2 = (bf16[16,3584]{1,0:T(8,128)(2,1)S(1)}, bf16[16,3584]{1,0:T(8,128)(2,1)S(1)}, u32[]{:S(2)}, u32[]{:S(2)}) collective-permute-start(bf16[16,3584]{1,0:T(8,128)(2,1)S(1)} %get-tuple-element.21), channel_id=1, source_target_pairs={{0,7},{1,0},{2,1},{3,2},{4,3},{5,4},{6,5},{7,6},{8,15},{9,8},{10,9... | collective-permute-start | bytes 344072 | tf_op jit(solution)/shard_map/ppermute | solution.py:185
  46.8 5.1 %collective-permute-start.6 = (bf16[16,3584]{1,0:T(8,128)(2,1)S(1)}, bf16[16,3584]{1,0:T(8,128)(2,1)S(1)}, u32[]{:S(2)}, u32[]{:S(2)}) collective-permute-start(bf16[16,3584]{1,0:T(8,128)(2,1)S(1)} %collective-permute-done.5), channel_id=1, source_target_pairs={{0,1},{1,2},{2,3},{3,4},{4,5},{5,6},{6,7},{7,0},{8,9},{9,10},{10,1... | collective-permute-start | bytes 344072 | tf_op jit(solution)/shard_map/ppermute | solution.py:185
  46.8 5.1 %collective-permute-start.3 = (bf16[16,3584]{1,0:T(8,128)(2,1)S(1)}, bf16[16,3584]{1,0:T(8,128)(2,1)S(1)}, u32[]{:S(2)}, u32[]{:S(2)}) collective-permute-start(bf16[16,3584]{1,0:T(8,128)(2,1)S(1)} %collective-permute-done.2), channel_id=1, source_target_pairs={{0,7},{1,0},{2,1},{3,2},{4,3},{5,4},{6,5},{7,6},{8,15},{9,8},{10,9... | collective-permute-start | bytes 344072 | tf_op jit(solution)/shard_map/ppermute | solution.py:185
  51.9 4.9 %collective-permute-start.7 = (bf16[16,3584]{1,0:T(8,128)(2,1)S(1)}, bf16[16,3584]{1,0:T(8,128)(2,1)S(1)}, u32[]{:S(2)}, u32[]{:S(2)}) collective-permute-start(bf16[16,3584]{1,0:T(8,128)(2,1)S(1)} %collective-permute-done.6), channel_id=1, source_target_pairs={{0,1},{1,2},{2,3},{3,4},{4,5},{5,6},{6,7},{7,0},{8,9},{9,10},{10,1... | collective-permute-start | bytes 344072 | tf_op jit(solution)/shard_map/ppermute | solution.py:185
  51.9 4.9 %collective-permute-start.4 = (bf16[16,3584]{1,0:T(8,128)(2,1)S(1)}, bf16[16,3584]{1,0:T(8,128)(2,1)S(1)}, u32[]{:S(2)}, u32[]{:S(2)}) collective-permute-start(bf16[16,3584]{1,0:T(8,128)(2,1)S(1)} %collective-permute-done.3), channel_id=1, source_target_pairs={{0,7},{1,0},{2,1},{3,2},{4,3},{5,4},{6,5},{7,6},{8,15},{9,8},{10,9... | collective-permute-start | bytes 344072 | tf_op jit(solution)/shard_map/ppermute | solution.py:185
  56.9 4.3 %collective-permute-start.8 = (bf16[8,3584]{1,0:T(8,128)(2,1)S(1)}, bf16[8,3584]{1,0:T(8,128)(2,1)S(1)}, u32[]{:S(2)}, u32[]{:S(2)}) collective-permute-start(bf16[8,3584]{1,0:T(8,128)(2,1)S(1)} %slice.59), channel_id=1, source_target_pairs={{0,1},{1,2},{2,3},{3,4},{4,5},{5,6},{6,7},{7,0},{8,9},{9,10},{10,1... | collective-permute-start | bytes 172040 | tf_op jit(solution)/shard_map/ppermute | solution.py:188
  56.9 4.3 %collective-permute-start.9 = (bf16[8,3584]{1,0:T(8,128)(2,1)S(1)}, bf16[8,3584]{1,0:T(8,128)(2,1)S(1)}, u32[]{:S(2)}, u32[]{:S(2)}) collective-permute-start(bf16[8,3584]{1,0:T(8,128)(2,1)S(1)} %slice.60), channel_id=1, source_target_pairs={{0,7},{1,0},{2,1},{3,2},{4,3},{5,4},{6,5},{7,6},{8,15},{9,8},{10,9... | collective-permute-start | bytes 172040 | tf_op jit(solution)/shard_map/ppermute | solution.py:188
  61.3 2.0 %copy-start.3 = (bf16[4608,384]{1,0:T(8,128)(2,1)S(1)}, bf16[4608,384]{1,0:T(8,128)(2,1)}, u32[]{:S(2)}) copy-start(bf16[4608,384]{1,0:T(8,128)(2,1)} %copy-done.2) | copy-start | bytes 10616836
  64.1 7.5 %collective-permute-start.19 = (bf16[64,2560]{1,0:T(8,128)(2,1)S(1)}, bf16[64,2560]{1,0:T(8,128)(2,1)S(1)}, u32[]{:S(2)}, u32[]{:S(2)}) collective-permute-start(bf16[64,2560]{1,0:T(8,128)(2,1)S(1)} %all_gather.3.refs_4_), channel_id=1, source_target_pairs={{0,1},{1,2},{2,3},{3,4},{4,5},{5,6},{6,7},{7,0},{8,9},{9,10},{10,1... | collective-permute-start | bytes 983048 | tf_op jit(solution)/shard_map/ppermute | solution.py:185
  64.2 10.1 %collective-permute-start.16 = (bf16[64,2560]{1,0:T(8,128)(2,1)S(1)}, bf16[64,2560]{1,0:T(8,128)(2,1)S(1)}, u32[]{:S(2)}, u32[]{:S(2)}) collective-permute-start(bf16[64,2560]{1,0:T(8,128)(2,1)S(1)} %all_gather.3.refs_4_), channel_id=1, source_target_pairs={{0,7},{1,0},{2,1},{3,2},{4,3},{5,4},{6,5},{7,6},{8,15},{9,8},{10,9... | collective-permute-start | bytes 983048 | tf_op jit(solution)/shard_map/ppermute | solution.py:185
  71.6 9.3 %collective-permute-start.20 = (bf16[64,2560]{1,0:T(8,128)(2,1)S(1)}, bf16[64,2560]{1,0:T(8,128)(2,1)S(1)}, u32[]{:S(2)}, u32[]{:S(2)}) collective-permute-start(bf16[64,2560]{1,0:T(8,128)(2,1)S(1)} %collective-permute-done.19.refs_11_), channel_id=1, source_target_pairs={{0,1},{1,2},{2,3},{3,4},{4,5},{5,6},{6,7},{7,0},{8,9},{9,10},{10,1... | collective-permute-start | bytes 983048 | tf_op jit(solution)/shard_map/ppermute | solution.py:185
  71.6 31.6 %collective-permute-start.25 = (bf16[1536,384]{1,0:T(8,128)(2,1)S(1)}, bf16[1536,384]{1,0:T(8,128)(2,1)S(1)}, u32[]{:S(2)}, u32[]{:S(2)}) collective-permute-start(bf16[1536,384]{1,0:T(8,128)(2,1)S(1)} %shard_map.48.refs_12_), channel_id=1, source_target_pairs={{0,64},{32,96},{64,128},{96,160},{128,192},{160,224},{192,0},{224,... | collective-permute-start | bytes 3538952 | tf_op jit(solution)/shard_map/ppermute | solution.py:185
  71.6 33.0 %collective-permute-start.24 = (bf16[1536,384]{1,0:T(8,128)(2,1)S(1)}, bf16[1536,384]{1,0:T(8,128)(2,1)S(1)}, u32[]{:S(2)}, u32[]{:S(2)}) collective-permute-start(bf16[1536,384]{1,0:T(8,128)(2,1)S(1)} %shard_map.48.refs_12_), channel_id=1, source_target_pairs={{0,192},{32,224},{64,0},{96,32},{128,64},{160,96},{192,128},{224,1... | collective-permute-start | bytes 3538952 | tf_op jit(solution)/shard_map/ppermute | solution.py:185
  74.3 9.8 %collective-permute-start.17 = (bf16[64,2560]{1,0:T(8,128)(2,1)S(1)}, bf16[64,2560]{1,0:T(8,128)(2,1)S(1)}, u32[]{:S(2)}, u32[]{:S(2)}) collective-permute-start(bf16[64,2560]{1,0:T(8,128)(2,1)S(1)} %collective-permute-done.16.refs_5_), channel_id=1, source_target_pairs={{0,7},{1,0},{2,1},{3,2},{4,3},{5,4},{6,5},{7,6},{8,15},{9,8},{10,9... | collective-permute-start | bytes 983048 | tf_op jit(solution)/shard_map/ppermute | solution.py:185
  76.9 21.4 %collective-permute-start.13 = (bf16[128,3584]{1,0:T(8,128)(2,1)S(1)}, bf16[128,3584]{1,0:T(8,128)(2,1)S(1)}, u32[]{:S(2)}, u32[]{:S(2)}) collective-permute-start(bf16[128,3584]{1,0:T(8,128)(2,1)S(1)} %constant_dynamic-update-slice_fusion.refs_0_), channel_id=1, source_target_pairs={{0,8},{8,16},{16,24},{24,0},{1,9},{9,17},{17,25},{25,1},{2,10},{10... | collective-permute-start | bytes 2752520 | tf_op jit(solution)/shard_map/ppermute | solution.py:185
  80.9 20.1 %collective-permute-start.12 = (bf16[128,3584]{1,0:T(8,128)(2,1)S(1)}, bf16[128,3584]{1,0:T(8,128)(2,1)S(1)}, u32[]{:S(2)}, u32[]{:S(2)}) collective-permute-start(bf16[128,3584]{1,0:T(8,128)(2,1)S(1)} %constant_dynamic-update-slice_fusion.refs_0_), channel_id=1, source_target_pairs={{0,24},{8,0},{16,8},{24,16},{1,25},{9,1},{17,9},{25,17},{2,26},{10... | collective-permute-start | bytes 2752520 | tf_op jit(solution)/shard_map/ppermute | solution.py:185
  84.0 7.6 %collective-permute-start.21 = (bf16[64,2560]{1,0:T(8,128)(2,1)S(1)}, bf16[64,2560]{1,0:T(8,128)(2,1)S(1)}, u32[]{:S(2)}, u32[]{:S(2)}) collective-permute-start(bf16[64,2560]{1,0:T(8,128)(2,1)S(1)} %collective-permute-done.20.refs_10_), channel_id=1, source_target_pairs={{0,1},{1,2},{2,3},{3,4},{4,5},{5,6},{6,7},{7,0},{8,9},{9,10},{10,1... | collective-permute-start | bytes 983048 | tf_op jit(solution)/shard_map/ppermute | solution.py:185
  91.6 6.2 %collective-permute-start.18 = (bf16[64,2560]{1,0:T(8,128)(2,1)S(1)}, bf16[64,2560]{1,0:T(8,128)(2,1)S(1)}, u32[]{:S(2)}, u32[]{:S(2)}) collective-permute-start(bf16[64,2560]{1,0:T(8,128)(2,1)S(1)} %collective-permute-done.17.refs_6_), channel_id=1, source_target_pairs={{0,7},{1,0},{2,1},{3,2},{4,3},{5,4},{6,5},{7,6},{8,15},{9,8},{10,9... | collective-permute-start | bytes 983048 | tf_op jit(solution)/shard_map/ppermute | solution.py:185
  97.8 7.8 %collective-permute-start.22 = (bf16[32,2560]{1,0:T(8,128)(2,1)S(1)}, bf16[32,2560]{1,0:T(8,128)(2,1)S(1)}, u32[]{:S(2)}, u32[]{:S(2)}) collective-permute-start(bf16[32,2560]{1,0:T(8,128)(2,1)S(1)} %slice.63), channel_id=1, source_target_pairs={{0,1},{1,2},{2,3},{3,4},{4,5},{5,6},{6,7},{7,0},{8,9},{9,10},{10,1... | collective-permute-start | bytes 491528 | tf_op jit(solution)/shard_map/ppermute | solution.py:188
  98.3 9.4 %collective-permute-start.23 = (bf16[32,2560]{1,0:T(8,128)(2,1)S(1)}, bf16[32,2560]{1,0:T(8,128)(2,1)S(1)}, u32[]{:S(2)}, u32[]{:S(2)}) collective-permute-start(bf16[32,2560]{1,0:T(8,128)(2,1)S(1)} %slice.64), channel_id=1, source_target_pairs={{0,7},{1,0},{2,1},{3,2},{4,3},{5,4},{6,5},{7,6},{8,15},{9,8},{10,9... | collective-permute-start | bytes 491528 | tf_op jit(solution)/shard_map/ppermute | solution.py:188
  100.9 9.3 %collective-permute-start.14 = (bf16[64,3584]{1,0:T(8,128)(2,1)S(1)}, bf16[64,3584]{1,0:T(8,128)(2,1)S(1)}, u32[]{:S(2)}, u32[]{:S(2)}) collective-permute-start(bf16[64,3584]{1,0:T(8,128)(2,1)S(1)} %slice.61), channel_id=1, source_target_pairs={{0,8},{8,16},{16,24},{24,0},{1,9},{9,17},{17,25},{25,1},{2,10},{10... | collective-permute-start | bytes 1376264 | tf_op jit(solution)/shard_map/ppermute | solution.py:188
  103.2 8.2 %collective-permute-start.15 = (bf16[64,3584]{1,0:T(8,128)(2,1)S(1)}, bf16[64,3584]{1,0:T(8,128)(2,1)S(1)}, u32[]{:S(2)}, u32[]{:S(2)}) collective-permute-start(bf16[64,3584]{1,0:T(8,128)(2,1)S(1)} %slice.62), channel_id=1, source_target_pairs={{0,24},{8,0},{16,8},{24,16},{1,25},{9,1},{17,9},{25,17},{2,26},{10... | collective-permute-start | bytes 1376264 | tf_op jit(solution)/shard_map/ppermute | solution.py:188
  104.6 10.0 %collective-permute-start.26 = (bf16[768,384]{1,0:T(8,128)(2,1)S(1)}, bf16[768,384]{1,0:T(8,128)(2,1)S(1)}, u32[]{:S(2)}, u32[]{:S(2)}) collective-permute-start(bf16[768,384]{1,0:T(8,128)(2,1)S(1)} %slice.65), channel_id=1, source_target_pairs={{0,64},{32,96},{64,128},{96,160},{128,192},{160,224},{192,0},{224,... | collective-permute-start | bytes 1769480 | tf_op jit(solution)/shard_map/ppermute | solution.py:188
  105.6 9.0 %collective-permute-start.27 = (bf16[768,384]{1,0:T(8,128)(2,1)S(1)}, bf16[768,384]{1,0:T(8,128)(2,1)S(1)}, u32[]{:S(2)}, u32[]{:S(2)}) collective-permute-start(bf16[768,384]{1,0:T(8,128)(2,1)S(1)} %slice.66), channel_id=1, source_target_pairs={{0,192},{32,224},{64,0},{96,32},{128,64},{160,96},{192,128},{224,1... | collective-permute-start | bytes 1769480 | tf_op jit(solution)/shard_map/ppermute | solution.py:188
  118.1 18.0 %collective-permute-start.28 = (f32[4,4,16,384]{3,2,1,0:T(8,128)S(1)}, f32[4,4,16,384]{3,2,1,0:T(8,128)S(1)}, u32[]{:S(2)}, u32[]{:S(2)}) collective-permute-start(f32[4,4,16,384]{3,2,1,0:T(8,128)S(1)} %slice_bitcast_fusion), channel_id=1, source_target_pairs={{0,32},{32,0},{64,96},{96,64},{128,160},{160,128},{192,224},{224,1... | collective-permute-start | bytes 1179656 | tf_op jit(solution)/shard_map/ppermute | solution.py:264

commit v2 on v0

--- a/solution.py
+++ b/solution.py
@@ -132,45 +132,35 @@
 
 
 def multiply(ny, nz, rows, *refs):
-    zs, ys, (b_ref, keep_ref, send_ref) = refs[:ny], refs[ny : ny + nz], refs[ny + nz :]
+    refs, (b_ref, keep_ref, send_ref) = refs[:-3], refs[-3:]
     group, y, z = lax.axis_index("grp"), lax.axis_index("row"), lax.axis_index("col")
     x, core = lax.div(group, 2), lax.rem(group, 2)
-    wide = zs[0].shape[1]
-    part = rows * nz // 2
-    for r in range(ny):
-        d = lax.rem(y + r - x + ny, ny)
-        out = jnp.dot(zs[r][...], b_ref[:wide, :], preferred_element_type=jnp.float32)
-        keep_ref[d] = jnp.where(core == 0, out[:part], out[part:])
-        send_ref[d] = jnp.where(core == 0, out[part:], out[:part])
-    for r in range(nz):
-        at = lax.rem(z + r, nz)
-        side = lax.div(at, nz // 2)
-        into = pl.ds(pl.multiple_of(lax.rem(at, nz // 2) * rows, rows), rows)
-        out = jnp.dot(ys[r][...], b_ref[wide:, :], preferred_element_type=jnp.float32)
-        for ref, here in ((keep_ref, side == core), (send_ref, side != core)):
-
-            @pl.when(here)
-            def _(ref=ref, out=out):
-                for q in range(ny):
-                    d = lax.rem(q - x + ny, ny)
-                    ref[d, into, :] += out[q * rows : (q + 1) * rows]
+    near = jnp.where(core == 0, 1, ny - 1)
+    far = ny - near
+    opposite = nz // 2
+    places = [[(0, 0), (2, 0)]]
+    for s in range(1, opposite):
+        places += [[(0, nz - s), (2, nz - s)], [(0, s), (2, s)]]
+    places += [[(0, opposite)], [(2, opposite)], [(near, 0), (far, 0)]]
+    for s in range(1, opposite):
+        places += [[(near, nz - s), (far, nz - s), (near, s), (far, s)]]
+    places += [[(near, opposite), (far, opposite)]]
+    for ref, held in zip(refs, places, strict=True):
+        out = jnp.dot(ref[...].reshape(len(held) * rows, ref.shape[-1]), b_ref[...], preferred_element_type=jnp.float32)
+        for i, (up_y, up_z) in enumerate(held):
+            d = lax.rem(y + up_y - x + ny, ny)
+            at = lax.rem(z + up_z, nz)
+            into = pl.ds(pl.multiple_of(lax.rem(at, nz // 2) * rows, rows), rows)
+            side = lax.div(at, nz // 2)
+            for to, here in ((keep_ref, side == core), (send_ref, side != core)):
+
+                @pl.when(here)
+                def _(to=to, out=out, i=i, d=d, into=into):
+                    to[d, into, :] = out[i * rows : (i + 1) * rows]
 
 
 def steps(n):
     return [(i, (i + 1) % n) for i in range(n)], [(i, (i - 1) % n) for i in range(n)]
-
-
-def ring(block, axis, n):
-    up, down = steps(n)
-    out = [block] * n
-    a = b = block
-    for s in range(1, n // 2):
-        a, b = lax.ppermute(a, axis, up), lax.ppermute(b, axis, down)
-        out[n - s], out[s] = a, b
-    h = block.shape[0] // 2
-    ta, tb = lax.ppermute(a[:h], axis, up), lax.ppermute(b[h:], axis, down)
-    out[n // 2] = jnp.concatenate([ta, tb], axis=0)
-    return out
 
 
 def body(amplitudes, integrals, block_tiles, assign):
@@ -180,7 +170,6 @@
     ny, nz = lax.axis_size("row"), lax.axis_size("col")
     own = 12
     wide = own * TP
-    split = 7 * TP
     small = [pltpu.SMEM((groups,), jnp.int32)] * 2
     swap = [(g, g ^ 1) for g in range(groups)]
     up = [(g, (g + 2) % groups) for g in range(groups)]
@@ -208,8 +197,22 @@
         scratch_shapes=small,
         compiler_params=limit,
     )(block_tiles, assign, mine, other)
+
+    across = [(y, (y + 2) % ny) for y in range(ny)]
+    z_up, z_down = steps(nz)
+    beside = [(g * ny + y, g * ny + (y - 1 + 2 * (g % 2)) % ny) for g in range(groups) for y in range(ny)]
+    pair = jnp.stack([piece, lax.ppermute(piece, "row", across)])
+    pair, to_right, to_left = lax.optimization_barrier((pair, to_right, to_left))
     from_left = lax.ppermute(to_right, "grp", up)
     from_right = lax.ppermute(to_left, "grp", down)
+    a = b = pair
+    parts, swapped = [pair], [lax.ppermute(pair, ("grp", "row"), beside)]
+    for s in range(1, nz // 2):
+        a, b = lax.ppermute(a, "col", z_up), lax.ppermute(b, "col", z_down)
+        parts += [a, b]
+        swapped.append(lax.ppermute(jnp.concatenate([a, b]), ("grp", "row"), beside))
+    ta, tb = lax.ppermute(a[0], "col", z_up), lax.ppermute(b[1], "col", z_down)
+    swapped.append(lax.ppermute(jnp.stack([ta, tb]), ("grp", "row"), beside))
     held = pl.pallas_call(
         functools.partial(join_tiles, groups, own),
         out_shape=sends,
@@ -218,20 +221,17 @@
         scratch_shapes=small,
         compiler_params=limit,
     )(block_tiles, assign, mine, other, from_left, from_right)
-
-    y_line = lax.all_gather(piece[:, split:], "row", axis=0, tiled=True)
-    z_line = lax.all_gather(piece[:, :split], "col", axis=0, tiled=True)
-    zs = ring(z_line, "row", ny)
-    ys = ring(y_line, "col", nz)
+    pieces = parts + [ta, tb] + swapped
+
     half_rows = rows * nz // 2
     kept = jax.ShapeDtypeStruct((ny, half_rows, cols), jnp.float32)
     keep, send = pl.pallas_call(
         functools.partial(multiply, ny, nz, rows),
         out_shape=(kept, kept),
-        in_specs=[VMEM] * (ny + nz + 1),
+        in_specs=[VMEM] * (len(pieces) + 1),
         out_specs=(VMEM, VMEM),
         compiler_params=pltpu.CompilerParams(vmem_limit_bytes=32 * 2**20),
-    )(*zs, *ys, held)
+    )(*pieces, held)
 
     p = keep + lax.ppermute(send, "grp", swap)
     h = half_rows // 2

time: 150 us -> 144 us (0.960)
  blocking collectives: 61 us -> 24.6 us
  waiting for transfers between devices: 33.7 us -> 67.8 us
  starting transfers between devices: 39.8 us -> 35.9 us
  Pallas kernels: 12.6 us -> 10.4 us
  local copies, waits for them, and re-layouts: 0.19 us -> 2.08 us
    all_gather x2 -> x0, blocking collectives: 36.3 us -> none  [the longest x1 26.3 us: body(): z_line = lax.all_gather(piece[:, :split], 'col', axis=0, tiled=True)]
    ppermute x12 -> x14, waiting for transfers between devices: 18.2 us -> 45.7 us  [the longest x1 20.1 us: body(): parts, swapped = ([pair], [lax.ppermute(pair, ('grp', 'row'), beside)])]
    ppermute x1, starting transfers between devices: 12.6 us -> 4.54 us  [body(): p = keep + lax.ppermute(send, 'grp', swap)]
    ppermute x1, waiting for transfers between devices: 0.01 us -> 6.55 us  [body(): from_left = lax.ppermute(to_right, 'grp', up)]
    ppermute x12 -> x14, starting transfers between devices: 15.5 us -> 19.9 us  [the longest x6 9.7 us: body(): a, b = (lax.ppermute(a, 'col', z_up), lax.ppermute(b, 'col', z_down))]
    unnamed x6, local copies, waits for them, and re-layouts: 0.01 us -> 2 us
  transfers between devices with their start and end apart: 20 -> 22, of which waited for: 8 -> 11; matrix products, arithmetic and copies ran while one was open for 0% -> 0% of each run, Pallas kernels for 3% -> 3%
where the time goes in v2:
time: 144 us; the launch traced here: 142 us
  waiting for transfers between devices  67.8 us (47%)
  starting transfers between devices  35.9 us (25%)
  blocking collectives  24.6 us (17%)
  Pallas kernels  10.4 us (7%)
  local copies, waits for them, and re-layouts  2.08 us (1%)
  other arithmetic  1.47 us (1%)
    ppermute x1, waiting for transfers between devices, body(): parts, swapped = ([pair], [lax.ppermute(pair, ('grp', 'row'), beside)])  20.1 us
    ppermute x6, waiting for transfers between devices, body(): a, b = (lax.ppermute(a, 'col', z_up), lax.ppermute(b, 'col', z_down))  15.9 us
    all_to_all x1, blocking collectives, body(): lax.all_to_all(amplitudes[0].reshape(groups, rows // groups, cap), 'grp',...  14.7 us
    all_to_all x1, blocking collectives, body(): piece = lax.all_to_all(packed, 'grp', 0, 0, tiled=True).reshape(rows, wide)  9.92 us
    ppermute x6, starting transfers between devices, body(): a, b = (lax.ppermute(a, 'col', z_up), lax.ppermute(b, 'col', z_down))  9.7 us
    ppermute x1, waiting for transfers between devices, body(): a = lax.ppermute(jnp.concatenate([p[2, :h], p[1, h:]]), 'grp', up)  8.76 us
    ppermute x1, waiting for transfers between devices, body(): from_left = lax.ppermute(to_right, 'grp', up)  6.55 us
    pallas_call x1, Pallas kernels, body(): pl.pallas_call(functools.partial(multiply, ny, nz, rows), out_shape=(kept...  6 us
  transfers between devices with their start and end apart: 22, of which 11 were waited for; matrix products, arithmetic and copies ran while one was open for 0% of the time, Pallas kernels for 3%

profile of v2, /device:TPU:1, one launch (start us, length us, event | category | flops | bytes accessed | tf_op | source)
XLA Modules:
  0.0 142.4 jit_solution(5949728885083516581)
XLA Ops:
  0.0 3.2 %collective-permute-start.1 = (bf16[4608,384]{1,0:T(8,128)(2,1)}, bf16[4608,384]{1,0:T(8,128)(2,1)S(1)}, u32[]{:S(2)}, u32[]{:S(2)}) collective-permute-start(bf16[4608,384]{1,0:T(8,128)(2,1)} %bitcast.33), channel_id=1, source_target_pairs={{0,32},{32,0},{64,96},{96,64},{128,160},{160,128},{192,224},{224,1... | collective-permute-start | bytes 10616840 | tf_op jit(solution)/shard_map/ppermute | solution.py:180
  3.2 0.0 copy-start.1
  3.2 0.0 copy-start.2
  3.2 14.7 %all_to_all.10.src_ref = bf16[8,8,4608]{2,1,0:T(8,128)(2,1)} all-to-all(bf16[8,8,4608]{2,1,0:T(8,128)(2,1)} %bitcast.40), channel_id=1, replica_groups=mesh['grp'=8,'row'=4,'col'=8] {'grp'}, dimensions={0} | all-to-all | bytes 1179648 | tf_op jit(solution)/shard_map/all_to_all | solution.py:181
  17.9 2.9 %shard_map.46 = bf16[8,8,1536]{2,1,0:T(8,128)(2,1)} custom-call(s32[8]{0:T(128)} %tiles_ref.5, s32[8]{0:T(128)} %assign_ref.5, bf16[8,8,4608]{2,1,0:T(8,128)(2,1)} %all_to_all.10.src_ref), custom_call_target="tpu_custom_call" | custom-call | tf_op jit(solution)/shard_map/pallas_call | solution.py:182
  20.8 9.9 %all_to_all.11 = bf16[8,8,1536]{2,1,0:T(8,128)(2,1)S(1)} all-to-all(bf16[8,8,1536]{2,1,0:T(8,128)(2,1)} %shard_map.46), channel_id=1, replica_groups=mesh['grp'=8,'row'=4,'col'=8] {'grp'}, dimensions={0} | all-to-all | bytes 393216 | tf_op jit(solution)/shard_map/all_to_all | solution.py:189
  30.7 1.5 %collective-permute-start = (bf16[64,1536]{1,0:T(8,128)(2,1)S(1)}, bf16[64,1536]{1,0:T(8,128)(2,1)S(1)}, u32[]{:S(2)}, u32[]{:S(2)}) collective-permute-start(bf16[64,1536]{1,0:T(8,128)(2,1)S(1)} %bitcast.38), channel_id=1, source_target_pairs={{0,16},{8,24},{16,0},{24,8},{1,17},{9,25},{17,1},{25,9},{2,18},{10... | collective-permute-start | bytes 589832 | tf_op jit(solution)/shard_map/ppermute | solution.py:204
  32.2 5.4 %collective-permute-done = bf16[64,1536]{1,0:T(8,128)(2,1)S(1)} collective-permute-done((bf16[64,1536]{1,0:T(8,128)(2,1)S(1)}, bf16[64,1536]{1,0:T(8,128)(2,1)S(1)}, u32[]{:S(2)}, u32[]{:S(2)}) %collective-permute-start) | collective-permute-done | bytes 196640 | tf_op jit(solution)/shard_map/ppermute | solution.py:204
  37.7 0.0 collective-permute-done.1.other_ref
  37.7 0.0 copy-done.1
  37.7 0.0 copy-done.2
  37.7 0.0 copy-start
  37.7 2.0 %copy-done = bf16[1,4608,384]{2,1,0:T(8,128)(2,1)S(1)} copy-done((bf16[1,4608,384]{2,1,0:T(8,128)(2,1)S(1)}, bf16[1,4608,384]{2,1,0:T(8,128)(2,1)}, u32[]{:S(2)}) %copy-start) | copy-done | bytes 3538968
  39.7 0.7 shard_map.47
  40.4 0.3 collective-permute-start.2
  40.8 4.0 %collective-permute-start.3 = (bf16[2,64,1536]{2,1,0:T(8,128)(2,1)S(1)}, bf16[2,64,1536]{2,1,0:T(8,128)(2,1)S(1)}, u32[]{:S(2)}, u32[]{:S(2)}) collective-permute-start(bf16[2,64,1536]{2,1,0:T(8,128)(2,1)S(1)} %pad_maximum_fusion.3.refs_0_), channel_id=1, source_target_pairs={{0,7},{1,0},{2,1},{3,2},{4,3},{5,4},{6,5},{7,6},{8,15},{9,8},{10,9... | collective-permute-start | bytes 1179656 | tf_op jit(solution)/shard_map/ppermute | solution.py:211
  44.8 7.5 %collective-permute-done.2.refs_1_ = bf16[2,64,1536]{2,1,0:T(8,128)(2,1)S(1)} collective-permute-done((bf16[2,64,1536]{2,1,0:T(8,128)(2,1)S(1)}, bf16[2,64,1536]{2,1,0:T(8,128)(2,1)S(1)}, u32[]{:S(2)}, u32[]{:S(2)}) %collective-permute-start.2) | collective-permute-done | bytes 393248 | tf_op jit(solution)/shard_map/ppermute | solution.py:211
  52.2 0.0 collective-permute-start.4
  52.2 0.0 collective-permute-done.3.refs_2_
  52.2 2.7 %collective-permute-start.5 = (bf16[2,64,1536]{2,1,0:T(8,128)(2,1)S(1)}, bf16[2,64,1536]{2,1,0:T(8,128)(2,1)S(1)}, u32[]{:S(2)}, u32[]{:S(2)}) collective-permute-start(bf16[2,64,1536]{2,1,0:T(8,128)(2,1)S(1)} %collective-permute-done.3.refs_2_), channel_id=1, source_target_pairs={{0,7},{1,0},{2,1},{3,2},{4,3},{5,4},{6,5},{7,6},{8,15},{9,8},{10,9... | collective-permute-start | bytes 1179656 | tf_op jit(solution)/shard_map/ppermute | solution.py:211
  54.9 0.3 collective-permute-start.15
  55.2 2.4 %collective-permute-start.16 = (bf16[1536,384]{1,0:T(8,128)(2,1)S(1)}, bf16[1536,384]{1,0:T(8,128)(2,1)S(1)}, u32[]{:S(2)}, u32[]{:S(2)}) collective-permute-start(bf16[1536,384]{1,0:T(8,128)(2,1)S(1)} %get-tuple-element.16), channel_id=1, source_target_pairs={{0,192},{32,224},{64,0},{96,32},{128,64},{160,96},{192,128},{224,1... | collective-permute-start | bytes 3538952 | tf_op jit(solution)/shard_map/ppermute | solution.py:207
  57.6 3.9 %collective-permute-done.4.refs_3_ = bf16[2,64,1536]{2,1,0:T(8,128)(2,1)S(1)} collective-permute-done((bf16[2,64,1536]{2,1,0:T(8,128)(2,1)S(1)}, bf16[2,64,1536]{2,1,0:T(8,128)(2,1)S(1)}, u32[]{:S(2)}, u32[]{:S(2)}) %collective-permute-start.4) | collective-permute-done | bytes 393248 | tf_op jit(solution)/shard_map/ppermute | solution.py:211
  61.5 0.0 collective-permute-start.6
  61.5 0.1 pad_maximum_fusion
  61.6 1.4 collective-permute-start.11
  63.0 0.0 collective-permute-done.5.refs_4_
  63.0 2.7 %collective-permute-start.7 = (bf16[2,64,1536]{2,1,0:T(8,128)(2,1)S(1)}, bf16[2,64,1536]{2,1,0:T(8,128)(2,1)S(1)}, u32[]{:S(2)}, u32[]{:S(2)}) collective-permute-start(bf16[2,64,1536]{2,1,0:T(8,128)(2,1)S(1)} %collective-permute-done.5.refs_4_), channel_id=1, source_target_pairs={{0,7},{1,0},{2,1},{3,2},{4,3},{5,4},{6,5},{7,6},{8,15},{9,8},{10,9... | collective-permute-start | bytes 1179656 | tf_op jit(solution)/shard_map/ppermute | solution.py:211
  65.7 0.1 pad_maximum_fusion.1
  65.7 4.2 %collective-permute-done.6.refs_5_ = bf16[2,64,1536]{2,1,0:T(8,128)(2,1)S(1)} collective-permute-done((bf16[2,64,1536]{2,1,0:T(8,128)(2,1)S(1)}, bf16[2,64,1536]{2,1,0:T(8,128)(2,1)S(1)}, u32[]{:S(2)}, u32[]{:S(2)}) %collective-permute-start.6) | collective-permute-done | bytes 393248 | tf_op jit(solution)/shard_map/ppermute | solution.py:211
  69.9 0.1 collective-permute-start.8
  70.0 0.4 collective-permute-done.7.refs_6_
  70.4 3.5 %collective-permute-start.9 = (bf16[64,1536]{1,0:T(8,128)(2,1)S(1)}, bf16[64,1536]{1,0:T(8,128)(2,1)S(1)}, u32[]{:S(2)}, u32[]{:S(2)}) collective-permute-start(bf16[64,1536]{1,0:T(8,128)(2,1)S(1)} %slice_bitcast_fusion.7), channel_id=1, source_target_pairs={{0,7},{1,0},{2,1},{3,2},{4,3},{5,4},{6,5},{7,6},{8,15},{9,8},{10,9... | collective-permute-start | bytes 589832 | tf_op jit(solution)/shard_map/ppermute | solution.py:214
  73.9 0.1 pad_maximum_fusion.2
  74.0 6.5 %collective-permute-done.15.fl_ref = bf16[1536,384]{1,0:T(8,128)(2,1)S(1)} collective-permute-done((bf16[1536,384]{1,0:T(8,128)(2,1)S(1)}, bf16[1536,384]{1,0:T(8,128)(2,1)S(1)}, u32[]{:S(2)}, u32[]{:S(2)}) %collective-permute-start.15) | collective-permute-done | bytes 1179680 | tf_op jit(solution)/shard_map/ppermute | solution.py:206
  80.5 1.3 collective-permute-start.12
  81.8 0.0 collective-permute-done.8.refs_7_
  81.8 1.3 collective-permute-start.13
  83.1 0.0 collective-permute-done.9.refs_8_
  83.1 1.0 collective-permute-start.10
  84.2 0.0 collective-permute-done.16.fr_ref
  84.2 0.2 collective-permute-start.14
  84.3 0.8 shard_map.48.refs_14_
  85.1 20.1 %collective-permute-done.10.refs_9_ = bf16[2,64,1536]{2,1,0:T(8,128)(2,1)S(1)} collective-permute-done((bf16[2,64,1536]{2,1,0:T(8,128)(2,1)S(1)}, bf16[2,64,1536]{2,1,0:T(8,128)(2,1)S(1)}, u32[]{:S(2)}, u32[]{:S(2)}) %collective-permute-start.10) | collective-permute-done | bytes 393248 | tf_op jit(solution)/shard_map/ppermute | solution.py:209
  105.3 0.0 collective-permute-done.11.refs_10_
  105.3 0.0 collective-permute-done.12.refs_11_
  105.3 4.2 %collective-permute-done.14.refs_13_ = bf16[2,64,1536]{2,1,0:T(8,128)(2,1)S(1)} collective-permute-done((bf16[2,64,1536]{2,1,0:T(8,128)(2,1)S(1)}, bf16[2,64,1536]{2,1,0:T(8,128)(2,1)S(1)}, u32[]{:S(2)}, u32[]{:S(2)}) %collective-permute-start.14) | collective-permute-done | bytes 393248 | tf_op jit(solution)/shard_map/ppermute | solution.py:215
  109.5 0.0 collective-permute-done.13.refs_12_
  109.5 6.0 %shard_map.49 = (f32[4,256,384]{2,1,0:T(8,128)S(1)}, f32[4,256,384]{2,1,0:T(8,128)S(1)}) custom-call(bf16[2,64,1536]{2,1,0:T(8,128)(2,1)S(1)} %pad_maximum_fusion.3.refs_0_, bf16[2,64,1536]{2,1,0:T(8,128)(2,1)S(1)} %collective-permute-done.2.refs_1_, bf16[2,64,1536]{2,1,0:T(8,128)(2,1)S(1)} %collective-permute-done.3.refs_2_, ...), custom_call_target="tpu_custom_call" | custom-call | tf_op jit(solution)/shard_map/pallas_call | solution.py:228
  115.5 4.5 %collective-permute-start.17 = (f32[4,256,384]{2,1,0:T(8,128)S(1)}, f32[4,256,384]{2,1,0:T(8,128)S(1)}, u32[]{:S(2)}, u32[]{:S(2)}) collective-permute-start(f32[4,256,384]{2,1,0:T(8,128)S(1)} %get-tuple-element.18), channel_id=1, source_target_pairs={{0,32},{32,0},{64,96},{96,64},{128,160},{160,128},{192,224},{224,1... | collective-permute-start | bytes 4718600 | tf_op jit(solution)/shard_map/ppermute | solution.py:236
  120.0 3.0 %collective-permute-done.17 = f32[4,256,384]{2,1,0:T(8,128)S(1)} collective-permute-done((f32[4,256,384]{2,1,0:T(8,128)S(1)}, f32[4,256,384]{2,1,0:T(8,128)S(1)}, u32[]{:S(2)}, u32[]{:S(2)}) %collective-permute-start.17) | collective-permute-done | bytes 1572896 | tf_op jit(solution)/shard_map/ppermute | solution.py:236
  123.1 0.3 add.15
  123.3 0.1 slice_bitcast_fusion.3
  123.4 0.1 collective-permute-start.18
  123.5 2.7 %collective-permute-start.20 = (f32[256,384]{1,0:T(8,128)S(1)}, f32[256,384]{1,0:T(8,128)S(1)}, u32[]{:S(2)}, u32[]{:S(2)}) collective-permute-start(f32[256,384]{1,0:T(8,128)S(1)} %pad_maximum_fusion.6), channel_id=1, source_target_pairs={{0,192},{32,224},{64,0},{96,32},{128,64},{160,96},{192,128},{224,1... | collective-permute-start | bytes 1179656 | tf_op jit(solution)/shard_map/ppermute | solution.py:239
  126.3 8.8 %collective-permute-done.18 = f32[256,384]{1,0:T(8,128)S(1)} collective-permute-done((f32[256,384]{1,0:T(8,128)S(1)}, f32[256,384]{1,0:T(8,128)S(1)}, u32[]{:S(2)}, u32[]{:S(2)}) %collective-permute-start.18) | collective-permute-done | bytes 393248 | tf_op jit(solution)/shard_map/ppermute | solution.py:238
  135.0 0.0 collective-permute-done.20
  135.0 0.1 slice_add_fusion
  135.1 0.1 collective-permute-start.19
  135.2 2.7 %collective-permute-start.21 = (f32[128,384]{1,0:T(8,128)S(1)}, f32[128,384]{1,0:T(8,128)S(1)}, u32[]{:S(2)}, u32[]{:S(2)}) collective-permute-start(f32[128,384]{1,0:T(8,128)S(1)} %get-tuple-element.19), channel_id=1, source_target_pairs={{0,192},{32,224},{64,0},{96,32},{128,64},{160,96},{192,128},{224,1... | collective-permute-start | bytes 589832 | tf_op jit(solution)/shard_map/ppermute | solution.py:241
  137.9 3.7 %collective-permute-done.19 = f32[128,384]{1,0:T(8,128)S(1)} collective-permute-done((f32[128,384]{1,0:T(8,128)S(1)}, f32[128,384]{1,0:T(8,128)S(1)}, u32[]{:S(2)}, u32[]{:S(2)}) %collective-permute-start.19) | collective-permute-done | bytes 196640 | tf_op jit(solution)/shard_map/ppermute | solution.py:240
  141.6 0.0 collective-permute-done.21
  141.6 0.8 fusion.1
  (6 shorter events, 0.2 us)
Async XLA Ops:
  0.0 37.7 %collective-permute-start.1 = (bf16[4608,384]{1,0:T(8,128)(2,1)}, bf16[4608,384]{1,0:T(8,128)(2,1)S(1)}, u32[]{:S(2)}, u32[]{:S(2)}) collective-permute-start(bf16[4608,384]{1,0:T(8,128)(2,1)} %bitcast.33), channel_id=1, source_target_pairs={{0,32},{32,0},{64,96},{96,64},{128,160},{160,128},{192,224},{224,1... | collective-permute-start | bytes 10616840 | tf_op jit(solution)/shard_map/ppermute | solution.py:180
  3.2 34.5 %copy-start.1 = (s32[8]{0:T(128)S(1)}, s32[8]{0:T(128)}, u32[]{:S(2)}) copy-start(s32[8]{0:T(128)} %tiles_ref.5) | copy-start | bytes 100
  3.2 34.5 %copy-start.2 = (s32[8]{0:T(128)S(1)}, s32[8]{0:T(128)}, u32[]{:S(2)}) copy-start(s32[8]{0:T(128)} %assign_ref.5) | copy-start | bytes 100
  30.7 7.0 %collective-permute-start = (bf16[64,1536]{1,0:T(8,128)(2,1)S(1)}, bf16[64,1536]{1,0:T(8,128)(2,1)S(1)}, u32[]{:S(2)}, u32[]{:S(2)}) collective-permute-start(bf16[64,1536]{1,0:T(8,128)(2,1)S(1)} %bitcast.38), channel_id=1, source_target_pairs={{0,16},{8,24},{16,0},{24,8},{1,17},{9,25},{17,1},{25,9},{2,18},{10... | collective-permute-start | bytes 589832 | tf_op jit(solution)/shard_map/ppermute | solution.py:204
  37.7 2.0 %copy-start = (bf16[1,4608,384]{2,1,0:T(8,128)(2,1)S(1)}, bf16[1,4608,384]{2,1,0:T(8,128)(2,1)}, u32[]{:S(2)}) copy-start(bf16[1,4608,384]{2,1,0:T(8,128)(2,1)} %param.5) | copy-start | bytes 10616836
  40.4 11.8 %collective-permute-start.2 = (bf16[2,64,1536]{2,1,0:T(8,128)(2,1)S(1)}, bf16[2,64,1536]{2,1,0:T(8,128)(2,1)S(1)}, u32[]{:S(2)}, u32[]{:S(2)}) collective-permute-start(bf16[2,64,1536]{2,1,0:T(8,128)(2,1)S(1)} %pad_maximum_fusion.3.refs_0_), channel_id=1, source_target_pairs={{0,1},{1,2},{2,3},{3,4},{4,5},{5,6},{6,7},{7,0},{8,9},{9,10},{10,1... | collective-permute-start | bytes 1179656 | tf_op jit(solution)/shard_map/ppermute | solution.py:211
  40.8 11.5 %collective-permute-start.3 = (bf16[2,64,1536]{2,1,0:T(8,128)(2,1)S(1)}, bf16[2,64,1536]{2,1,0:T(8,128)(2,1)S(1)}, u32[]{:S(2)}, u32[]{:S(2)}) collective-permute-start(bf16[2,64,1536]{2,1,0:T(8,128)(2,1)S(1)} %pad_maximum_fusion.3.refs_0_), channel_id=1, source_target_pairs={{0,7},{1,0},{2,1},{3,2},{4,3},{5,4},{6,5},{7,6},{8,15},{9,8},{10,9... | collective-permute-start | bytes 1179656 | tf_op jit(solution)/shard_map/ppermute | solution.py:211
  52.2 9.3 %collective-permute-start.4 = (bf16[2,64,1536]{2,1,0:T(8,128)(2,1)S(1)}, bf16[2,64,1536]{2,1,0:T(8,128)(2,1)S(1)}, u32[]{:S(2)}, u32[]{:S(2)}) collective-permute-start(bf16[2,64,1536]{2,1,0:T(8,128)(2,1)S(1)} %collective-permute-done.2.refs_1_), channel_id=1, source_target_pairs={{0,1},{1,2},{2,3},{3,4},{4,5},{5,6},{6,7},{7,0},{8,9},{9,10},{10,1... | collective-permute-start | bytes 1179656 | tf_op jit(solution)/shard_map/ppermute | solution.py:211
  52.2 10.7 %collective-permute-start.5 = (bf16[2,64,1536]{2,1,0:T(8,128)(2,1)S(1)}, bf16[2,64,1536]{2,1,0:T(8,128)(2,1)S(1)}, u32[]{:S(2)}, u32[]{:S(2)}) collective-permute-start(bf16[2,64,1536]{2,1,0:T(8,128)(2,1)S(1)} %collective-permute-done.3.refs_2_), channel_id=1, source_target_pairs={{0,7},{1,0},{2,1},{3,2},{4,3},{5,4},{6,5},{7,6},{8,15},{9,8},{10,9... | collective-permute-start | bytes 1179656 | tf_op jit(solution)/shard_map/ppermute | solution.py:211
  54.9 25.6 %collective-permute-start.15 = (bf16[1536,384]{1,0:T(8,128)(2,1)S(1)}, bf16[1536,384]{1,0:T(8,128)(2,1)S(1)}, u32[]{:S(2)}, u32[]{:S(2)}) collective-permute-start(bf16[1536,384]{1,0:T(8,128)(2,1)S(1)} %get-tuple-element.15), channel_id=1, source_target_pairs={{0,64},{32,96},{64,128},{96,160},{128,192},{160,224},{192,0},{224,... | collective-permute-start | bytes 3538952 | tf_op jit(solution)/shard_map/ppermute | solution.py:206
  55.2 29.0 %collective-permute-start.16 = (bf16[1536,384]{1,0:T(8,128)(2,1)S(1)}, bf16[1536,384]{1,0:T(8,128)(2,1)S(1)}, u32[]{:S(2)}, u32[]{:S(2)}) collective-permute-start(bf16[1536,384]{1,0:T(8,128)(2,1)S(1)} %get-tuple-element.16), channel_id=1, source_target_pairs={{0,192},{32,224},{64,0},{96,32},{128,64},{160,96},{192,128},{224,1... | collective-permute-start | bytes 3538952 | tf_op jit(solution)/shard_map/ppermute | solution.py:207
  61.5 8.4 %collective-permute-start.6 = (bf16[2,64,1536]{2,1,0:T(8,128)(2,1)S(1)}, bf16[2,64,1536]{2,1,0:T(8,128)(2,1)S(1)}, u32[]{:S(2)}, u32[]{:S(2)}) collective-permute-start(bf16[2,64,1536]{2,1,0:T(8,128)(2,1)S(1)} %collective-permute-done.4.refs_3_), channel_id=1, source_target_pairs={{0,1},{1,2},{2,3},{3,4},{4,5},{5,6},{6,7},{7,0},{8,9},{9,10},{10,1... | collective-permute-start | bytes 1179656 | tf_op jit(solution)/shard_map/ppermute | solution.py:211
  61.6 43.7 %collective-permute-start.11 = (bf16[4,64,1536]{2,1,0:T(8,128)(2,1)S(1)}, bf16[4,64,1536]{2,1,0:T(8,128)(2,1)S(1)}, u32[]{:S(2)}, u32[]{:S(2)}) collective-permute-start(bf16[4,64,1536]{2,1,0:T(8,128)(2,1)S(1)} %pad_maximum_fusion), channel_id=1, source_target_pairs={{0,24},{8,0},{16,8},{24,16},{32,40},{40,48},{48,56},{56,32},{64,88... | collective-permute-start | bytes 2359304 | tf_op jit(solution)/shard_map/ppermute | solution.py:213
  63.0 7.4 %collective-permute-start.7 = (bf16[2,64,1536]{2,1,0:T(8,128)(2,1)S(1)}, bf16[2,64,1536]{2,1,0:T(8,128)(2,1)S(1)}, u32[]{:S(2)}, u32[]{:S(2)}) collective-permute-start(bf16[2,64,1536]{2,1,0:T(8,128)(2,1)S(1)} %collective-permute-done.5.refs_4_), channel_id=1, source_target_pairs={{0,7},{1,0},{2,1},{3,2},{4,3},{5,4},{6,5},{7,6},{8,15},{9,8},{10,9... | collective-permute-start | bytes 1179656 | tf_op jit(solution)/shard_map/ppermute | solution.py:211
  69.9 11.9 %collective-permute-start.8 = (bf16[64,1536]{1,0:T(8,128)(2,1)S(1)}, bf16[64,1536]{1,0:T(8,128)(2,1)S(1)}, u32[]{:S(2)}, u32[]{:S(2)}) collective-permute-start(bf16[64,1536]{1,0:T(8,128)(2,1)S(1)} %slice_bitcast_fusion.8), channel_id=1, source_target_pairs={{0,1},{1,2},{2,3},{3,4},{4,5},{5,6},{6,7},{7,0},{8,9},{9,10},{10,1... | collective-permute-start | bytes 589832 | tf_op jit(solution)/shard_map/ppermute | solution.py:214
  70.4 12.7 %collective-permute-start.9 = (bf16[64,1536]{1,0:T(8,128)(2,1)S(1)}, bf16[64,1536]{1,0:T(8,128)(2,1)S(1)}, u32[]{:S(2)}, u32[]{:S(2)}) collective-permute-start(bf16[64,1536]{1,0:T(8,128)(2,1)S(1)} %slice_bitcast_fusion.7), channel_id=1, source_target_pairs={{0,7},{1,0},{2,1},{3,2},{4,3},{5,4},{6,5},{7,6},{8,15},{9,8},{10,9... | collective-permute-start | bytes 589832 | tf_op jit(solution)/shard_map/ppermute | solution.py:214
  80.5 24.8 %collective-permute-start.12 = (bf16[4,64,1536]{2,1,0:T(8,128)(2,1)S(1)}, bf16[4,64,1536]{2,1,0:T(8,128)(2,1)S(1)}, u32[]{:S(2)}, u32[]{:S(2)}) collective-permute-start(bf16[4,64,1536]{2,1,0:T(8,128)(2,1)S(1)} %pad_maximum_fusion.1), channel_id=1, source_target_pairs={{0,24},{8,0},{16,8},{24,16},{32,40},{40,48},{48,56},{56,32},{64,88... | collective-permute-start | bytes 2359304 | tf_op jit(solution)/shard_map/ppermute | solution.py:213
  81.8 27.7 %collective-permute-start.13 = (bf16[4,64,1536]{2,1,0:T(8,128)(2,1)S(1)}, bf16[4,64,1536]{2,1,0:T(8,128)(2,1)S(1)}, u32[]{:S(2)}, u32[]{:S(2)}) collective-permute-start(bf16[4,64,1536]{2,1,0:T(8,128)(2,1)S(1)} %pad_maximum_fusion.2), channel_id=1, source_target_pairs={{0,24},{8,0},{16,8},{24,16},{32,40},{40,48},{48,56},{56,32},{64,88... | collective-permute-start | bytes 2359304 | tf_op jit(solution)/shard_map/ppermute | solution.py:213
  83.1 22.2 %collective-permute-start.10 = (bf16[2,64,1536]{2,1,0:T(8,128)(2,1)S(1)}, bf16[2,64,1536]{2,1,0:T(8,128)(2,1)S(1)}, u32[]{:S(2)}, u32[]{:S(2)}) collective-permute-start(bf16[2,64,1536]{2,1,0:T(8,128)(2,1)S(1)} %pad_maximum_fusion.3.refs_0_), channel_id=1, source_target_pairs={{0,24},{8,0},{16,8},{24,16},{32,40},{40,48},{48,56},{56,32},{64,88... | collective-permute-start | bytes 1179656 | tf_op jit(solution)/shard_map/ppermute | solution.py:209
  84.2 25.3 %collective-permute-start.14 = (bf16[2,64,1536]{2,1,0:T(8,128)(2,1)S(1)}, bf16[2,64,1536]{2,1,0:T(8,128)(2,1)S(1)}, u32[]{:S(2)}, u32[]{:S(2)}) collective-permute-start(bf16[2,64,1536]{2,1,0:T(8,128)(2,1)S(1)} %pad_maximum_fusion.4), channel_id=1, source_target_pairs={{0,24},{8,0},{16,8},{24,16},{32,40},{40,48},{48,56},{56,32},{64,88... | collective-permute-start | bytes 1179656 | tf_op jit(solution)/shard_map/ppermute | solution.py:215
  115.5 7.6 %collective-permute-start.17 = (f32[4,256,384]{2,1,0:T(8,128)S(1)}, f32[4,256,384]{2,1,0:T(8,128)S(1)}, u32[]{:S(2)}, u32[]{:S(2)}) collective-permute-start(f32[4,256,384]{2,1,0:T(8,128)S(1)} %get-tuple-element.18), channel_id=1, source_target_pairs={{0,32},{32,0},{64,96},{96,64},{128,160},{160,128},{192,224},{224,1... | collective-permute-start | bytes 4718600 | tf_op jit(solution)/shard_map/ppermute | solution.py:236
  123.4 11.6 %collective-permute-start.18 = (f32[256,384]{1,0:T(8,128)S(1)}, f32[256,384]{1,0:T(8,128)S(1)}, u32[]{:S(2)}, u32[]{:S(2)}) collective-permute-start(f32[256,384]{1,0:T(8,128)S(1)} %pad_maximum_fusion.5), channel_id=1, source_target_pairs={{0,64},{32,96},{64,128},{96,160},{128,192},{160,224},{192,0},{224,... | collective-permute-start | bytes 1179656 | tf_op jit(solution)/shard_map/ppermute | solution.py:238
  123.5 11.5 %collective-permute-start.20 = (f32[256,384]{1,0:T(8,128)S(1)}, f32[256,384]{1,0:T(8,128)S(1)}, u32[]{:S(2)}, u32[]{:S(2)}) collective-permute-start(f32[256,384]{1,0:T(8,128)S(1)} %pad_maximum_fusion.6), channel_id=1, source_target_pairs={{0,192},{32,224},{64,0},{96,32},{128,64},{160,96},{192,128},{224,1... | collective-permute-start | bytes 1179656 | tf_op jit(solution)/shard_map/ppermute | solution.py:239
  135.1 6.5 %collective-permute-start.19 = (f32[128,384]{1,0:T(8,128)S(1)}, f32[128,384]{1,0:T(8,128)S(1)}, u32[]{:S(2)}, u32[]{:S(2)}) collective-permute-start(f32[128,384]{1,0:T(8,128)S(1)} %get-tuple-element.20), channel_id=1, source_target_pairs={{0,64},{32,96},{64,128},{96,160},{128,192},{160,224},{192,0},{224,... | collective-permute-start | bytes 589832 | tf_op jit(solution)/shard_map/ppermute | solution.py:240
  135.2 6.4 %collective-permute-start.21 = (f32[128,384]{1,0:T(8,128)S(1)}, f32[128,384]{1,0:T(8,128)S(1)}, u32[]{:S(2)}, u32[]{:S(2)}) collective-permute-start(f32[128,384]{1,0:T(8,128)S(1)} %get-tuple-element.19), channel_id=1, source_target_pairs={{0,192},{32,224},{64,0},{96,32},{128,64},{160,96},{192,128},{224,1... | collective-permute-start | bytes 589832 | tf_op jit(solution)/shard_map/ppermute | solution.py:241
